TPU v7x, 512 devices: a whole 4x4x16 slice. The times are simulated.
512 devices in a mesh: dp: 32 (over z, x_hi), point: 16 (over y, x_lo, core).
Axes of the slice: x: 4 (x_hi: 2, x_lo: 2; x = x_hi * 2 + x_lo), y: 4, z: 16, core: 2. Of those that a mesh axis runs over, the one named last changes fastest.
Arguments:
- points: bfloat16 [32, 2, 4096, 512], P('dp', None, 'point'), may hold values from -6 to 6
- hilbert_rank: int32 [32, 2, 4096], P('dp', None, 'point'), may hold values from 0 to 4095, as said below
- patch_id: int32 [32, 2, 4096], P('dp', None, 'point'), may hold values from 0 to 31, never falling along the last dimension, each value on 1 to 256 neighbouring positions
- w_qkv: bfloat16 [512, 1536], replicated, may hold values from -8 to 8
- w_out: bfloat16 [512, 512], replicated, may hold values from -0.25 to 0.25
- w_up: bfloat16 [2048, 512], P('point'), may hold values from -0.25 to 0.25
- w_down: bfloat16 [2048, 512], P('point'), may hold values from -0.125 to 0.125
- cotangent: bfloat16 [32, 2, 4096, 512], P('dp', None, 'point'), may hold values from -0.0234375 to 0.0234375
Outputs:
- layer_out: bfloat16 [32, 2, 4096, 512], P('dp', None, 'point')
- grad_down: float32 [2048, 512], P('point')
Inputs may be any that keep to these rules, and one draw needn't show every extreme that they name: `hilbert_rank`: within each cloud the values are a permutation of 0 to 4095. At most 32 points of one device's block of 256 points in Z order have their Hilbert position in one device's block; every Z block sends exactly 32 points to one Hilbert block. `patch_id`: patches are runs of 1 to 256 positions.
All inputs are finite; a program needn't handle non-finite values.
Results may differ from a plain program's by a relative error of at most 0.024.
Values may be sent and summed in bfloat16 or wider, within the bound.
No kernel may reach another device: no remote copies, remote signals or barrier semaphores. Data moves between devices by JAX's collectives and lax.ppermute only.
A program may use at most 64 MiB of HBM per device.

v0:
```python
import jax
import jax.numpy as jnp
from jax import lax
from jax.sharding import PartitionSpec as P

HEADS = 8
PATCH = 256


def extended(block, sides, width):
    for axis, dim in sides:
        count = lax.axis_size(axis)
        forward = [(i, i + 1) for i in range(count - 1)]
        backward = [(target, source) for source, target in forward]
        low = lax.ppermute(
            lax.slice_in_dim(block, block.shape[dim] - width, None, axis=dim), axis, forward
        )
        high = lax.ppermute(lax.slice_in_dim(block, 0, width, axis=dim), axis, backward)
        block = jnp.concatenate([low, block, high], axis=dim)
    return block


def normalize(values):
    wide = values.astype(jnp.float32)
    centre = jnp.mean(wide, axis=-1, keepdims=True)
    spread = jnp.mean(jnp.square(wide - centre), axis=-1, keepdims=True)
    return ((wide - centre) * lax.rsqrt(spread + 1e-05)).astype(jnp.bfloat16)


def attend(queries, query_tags, keyvals, key_tags):
    batch, length, width = queries.shape
    head_size = width // HEADS
    query_heads = queries.reshape(batch, length, HEADS, head_size)
    key_heads = keyvals[..., :width].reshape(batch, -1, HEADS, head_size)
    value_heads = keyvals[..., width:].reshape(batch, -1, HEADS, head_size)
    scores = jnp.einsum(
        "bqhd,bkhd->bhqk", query_heads, key_heads, preferred_element_type=jnp.float32
    ) * head_size ** (-0.5)
    allowed = query_tags[:, None, :, None] == key_tags[:, None, None, :]
    scores = jnp.where(allowed, scores, -1e30)
    peak = jnp.max(scores, axis=-1, keepdims=True)
    weights = jnp.where(allowed, jnp.exp(scores - peak), 0.0)
    total = jnp.sum(weights, axis=-1, keepdims=True)
    probs = (weights / total).astype(jnp.bfloat16)
    mixed = jnp.einsum("bhqk,bkhd->bqhd", probs, value_heads, preferred_element_type=jnp.float32)
    return mixed.reshape(batch, length, width).astype(jnp.bfloat16)


def fill_send(features, where_to, capacity):
    return jnp.zeros((capacity, features.shape[1]), features.dtype).at[where_to].set(features)


def fill_labels(labels, where_to, capacity, empty_mark):
    return jnp.full((capacity,), empty_mark, jnp.int32).at[where_to].set(labels)


def place_rows(arrived, places, length):
    return jnp.zeros((length, arrived.shape[1]), arrived.dtype).at[places].set(arrived, mode="drop")


def on_device(points, hilbert_rank, patch_id, w_qkv, w_out, w_up, w_down, cotangent):
    features = points[0]
    ranks = hilbert_rank[0]
    tags = patch_id[0] + 1
    clouds, length, width = features.shape
    devices = lax.axis_size("point")
    capacity = 2 * length // devices
    target = ranks // length
    local_rank = ranks - target * length
    one_hot = (target[..., None] == jnp.arange(devices, dtype=jnp.int32)).astype(jnp.int32)
    earlier = jnp.cumsum(one_hot, axis=1) - one_hot
    slot_index = jnp.sum(earlier * one_hot, axis=2)
    where_to = target * capacity + slot_index
    outgoing = jax.vmap(fill_send, in_axes=(0, 0, None))(features, where_to, devices * capacity)
    labels = jax.vmap(fill_labels, in_axes=(0, 0, None, None))(
        local_rank, where_to, devices * capacity, length
    )
    arrived, places = (
        lax.all_to_all(
            outgoing.reshape(clouds, devices, capacity, width),
            "point",
            split_axis=1,
            concat_axis=1,
            tiled=True,
        ),
        lax.all_to_all(
            labels.reshape(clouds, devices, capacity),
            "point",
            split_axis=1,
            concat_axis=1,
            tiled=True,
        ),
    )
    ordered = jax.vmap(place_rows, in_axes=(0, 0, None))(
        arrived.reshape(clouds, devices * capacity, width),
        places.reshape(clouds, devices * capacity),
        length,
    )
    rows_all = clouds * length
    normed = normalize(ordered)
    projected = jnp.dot(normed.reshape(rows_all, width), w_qkv, preferred_element_type=jnp.float32)
    projected = projected.astype(jnp.bfloat16).reshape(clouds, length, 3 * width)
    queries = projected[..., :width]
    keyvals = projected[..., width:]
    wide_kv, wide_tags = (
        extended(keyvals, (("point", 1),), PATCH),
        extended(tags, (("point", 1),), PATCH),
    )
    attended = attend(queries, tags, wide_kv, wide_tags)
    flat_in = ordered.reshape(rows_all, width)
    residual = (
        flat_in.astype(jnp.float32)
        + jnp.dot(attended.reshape(rows_all, width), w_out, preferred_element_type=jnp.float32)
    ).astype(jnp.bfloat16)
    normed_two = normalize(residual)
    product = lax.dot_general(
        normed_two,
        lax.all_gather(w_up, "point", axis=0, tiled=True),
        (((1,), (1,)), ((), ())),
        preferred_element_type=jnp.float32,
    )
    hidden = jax.nn.gelu(product).astype(jnp.bfloat16)
    mixed = jnp.dot(
        hidden,
        lax.all_gather(w_down, "point", axis=0, tiled=True),
        preferred_element_type=jnp.float32,
    )
    layer_out = (
        (residual.astype(jnp.float32) + mixed)
        .astype(jnp.bfloat16)
        .reshape(1, clouds, length, width)
    )
    cot_rows = cotangent[0].reshape(rows_all, width)
    grad_part = lax.psum_scatter(
        lax.dot_general(
            hidden, cot_rows, (((0,), (0,)), ((), ())), preferred_element_type=jnp.float32
        ).astype(jnp.bfloat16),
        "point",
        scatter_dimension=0,
        tiled=True,
    ).astype(jnp.float32)
    grad_down = lax.psum(grad_part, "dp")
    return (layer_out, grad_down)


def solution(mesh):
    placed = (
        P("dp", None, "point", None),
        P("dp", None, "point"),
        P("dp", None, "point"),
        P(),
        P(),
        P("point", None),
        P("point", None),
        P("dp", None, "point", None),
    )
    return jax.shard_map(
        on_device,
        mesh=mesh,
        in_specs=placed,
        out_specs=(P("dp", None, "point", None), P("point", None)),
        check_vma=False,
    )
```

profile of v0, /device:TPU:32, one launch (start us, length us, event | category | flops | bytes accessed | tf_op | source)
XLA Modules:
  0.0 400.5 jit_solution(17143095456123469292)
XLA Ops:
  7.2 0.0 copy-start
  7.2 0.0 all-gather.3.cloned.1.call-start
  7.2 0.7 all-gather.3.cloned.1.call-update
  7.9 0.7 squeeze.13
  8.6 1.2 reduce-window.6
  9.8 0.2 slice_reduce_fusion
  10.1 0.7 fusion.39
  10.8 0.1 fusion.34
  10.9 0.7 fusion.38
  11.6 24.5 %scatter_fusion = s32[2,512]{1,0:T(2,128)S(1)} fusion(s32[2,512]{1,0:T(2,128)S(1)} %broadcast.201, s32[512]{0:T(512)S(1)} %bitcast.91, s32[512]{0:T(512)S(1)} %bitcast.105), kind=kCustom, calls=%fused_computation | custom fusion | bytes 10240 | tf_op jit(solution)/shard_map/vmap()/scatter | solution.py:54
  36.1 0.1 reshape.229
  36.2 0.6 copy.26
  36.8 5.5 %all-to-all-start = ((s32[2,16,32]{2,0,1:T(2,128)}), s32[2,16,32]{2,0,1:T(2,128)S(1)}, u32[]{:S(2)}, u32[]{:S(2)}) async-start(s32[2,16,32]{2,0,1:T(2,128)} %copy.26), calls=%async_computation | async-start | bytes 32768 | tf_op jit(solution)/shard_map/all_to_all | solution.py:86
  42.3 0.1 broadcast_in_dim.38
  42.4 27.1 %scatter_fusion.1 = bf16[2,512,512]{2,1,0:T(8,128)(2,1)S(1)} fusion(bf16[2,512,512]{2,1,0:T(8,128)(2,1)S(1)} %broadcast_in_dim.38, s32[512]{0:T(512)S(1)} %bitcast.92, bf16[512,512]{1,0:T(8,128)(2,1)S(1)} %bitcast.101), kind=kCustom, calls=%fused_computation.1 | custom fusion | bytes 1576960 | tf_op jit(solution)/shard_map/vmap()/scatter | solution.py:50
  69.5 0.0 copy-start.5
  69.5 0.0 copy-start.6
  69.5 1.1 copy.28
  70.6 0.0 all-to-all-done
  70.6 5.7 %all-to-all-start.1 = ((bf16[2,16,32,512]{3,2,0,1:T(8,128)(2,1)}), bf16[2,16,32,512]{3,2,0,1:T(8,128)(2,1)S(1)}, u32[]{:S(2)}, u32[]{:S(2)}) async-start(bf16[2,16,32,512]{3,2,0,1:T(8,128)(2,1)} %copy.28), calls=%async_computation.1 | async-start | bytes 2097152 | tf_op jit(solution)/shard_map/all_to_all | solution.py:79
  76.3 0.0 all-gather.5.cloned.1.call-start
  76.4 0.1 reshape.230
  76.5 0.1 multiply_reduce_fusion.1
  76.6 0.1 and_reduce_fusion
  76.7 16.2 %all-to-all-done.1 = bf16[2,16,32,512]{3,2,0,1:T(8,128)(2,1)S(1)} async-done(((bf16[2,16,32,512]{3,2,0,1:T(8,128)(2,1)}), bf16[2,16,32,512]{3,2,0,1:T(8,128)(2,1)S(1)}, u32[]{:S(2)}, u32[]{:S(2)}) %all-to-all-start.1) | async-done | bytes 1048608 | tf_op jit(solution)/shard_map/all_to_all | solution.py:79
  92.9 1.1 copy.29
  94.0 5.6 %scatter_custom_fusion.2 = bf16[512,512]{1,0:T(8,128)(2,1)S(1)} fusion(s32[1024]{0:T(1024)S(1)} %bitcast.106, bf16[1024,512]{1,0:T(8,128)(2,1)} %bitcast.100, bf16[]{:T(256)} %constant.19.clone.1), kind=kCustom, calls=%fused_computation.44 | custom fusion | bytes 524800 | tf_op jit(solution)/shard_map/convert_element_type | solution.py:112
  99.6 0.1 convert_reduce_fusion.1
  99.8 0.3 multiply_reduce_fusion
  100.1 0.2 multiply_convert_fusion
  100.4 0.0 copy-start.4
  100.4 1.0 convolution_convert_fusion
  101.4 0.1 slice.30
  101.5 1.0 copy-done.1
  102.5 2.5 collective-permute-start
  105.1 1.3 collective-permute-start.1
  106.4 3.0 collective-permute-start.2
  109.4 1.3 collective-permute-start.3
  110.7 0.0 all-gather.5.cloned.1.call-update
  110.7 0.0 reduce-scatter.2.cloned.1.call-start
  110.8 0.0 collective-permute-done.2
  110.8 2.6 collective-permute-done.3
  113.4 0.3 broadcast_compare_fusion
  113.7 1.9 slice.32
  115.5 2.1 copy.31
  117.6 1.7 pad_maximum_fusion
  119.3 1.9 fusion.42
  121.2 2.7 copy.32
  123.8 2.6 copy.30
  126.4 11.4 %fusion.43 = (f32[2,8,256]{2,1,0:T(8,128)S(1)}, f32[2,8,256,768]{3,2,1,0:T(8,128)}) fusion(pred[2,256,768]{2,1,0:T(8,128)(4,1)S(1)} %broadcast_compare_fusion, bf16[2,256,8,64]{1,3,2,0:T(8,128)(2,1)S(1)} %bitcast.102, bf16[2,768,8,64]{1,3,2,0:T(8,128)(2,1)} %bitcast.96), kind=kOutput, calls=%fused_computation.93 | convolution fusion | flops 418382592 | bytes 15089664 | tf_op jit(solution)/shard_map/sub | solution.py:42
  137.8 7.3 %fusion.21 = bf16[2,256,8,64]{1,3,2,0:T(8,128)(2,1)S(1)} fusion(bf16[2,768,8,64]{1,3,2,0:T(8,128)(2,1)} %bitcast.97, f32[2,8,256,768]{3,2,1,0:T(8,128)} %get-tuple-element.7, f32[2,8,256]{2,1,0:T(8,128)S(1)} %get-tuple-element.6), kind=kOutput, calls=%fused_computation.34 | convolution fusion | flops 409206784 | bytes 14696448 | tf_op jit(solution)/shard_map/bhqk,bkhd->bqhd/dot_general | solution.py:45
  145.1 0.5 copy.33
  145.6 0.1 copy.38
  145.7 0.6 convert_reduce_fusion
  146.3 0.3 fusion.22
  146.6 0.0 all-gather.3.cloned.1.call-done
  146.7 3.6 fusion.13
  150.2 1.3 copy-done.9
  151.6 2.6 convolution_convert_fusion.1
  154.2 0.0 reduce-scatter.2.cloned.1.call-update
  154.2 4.4 %all-gather.5.cloned.1.call-done = bf16[2048,512]{1,0:T(8,128)(2,1)} async-done(((bf16[128,512]{1,0:T(8,128)(2,1)}), bf16[2048,512]{1,0:T(8,128)(2,1)}) %all-gather.5.cloned.1.call-update) | async-done | bytes 2097168 | tf_op jit(solution)/shard_map/all_gather | solution.py:125
  158.7 4.3 %fusion.16 = bf16[512,512]{1,0:T(8,128)(2,1)} fusion(bf16[512,2048]{1,0:T(8,128)(2,1)} %copy-done.9, bf16[2048,512]{1,0:T(8,128)(2,1)} %all-gather.5.cloned.1.call-done, bf16[512,512]{1,0:T(8,128)(2,1)S(1)} %get-tuple-element.9), kind=kOutput, calls=%fused_computation.30 | convolution fusion | flops 1074528256 | bytes 5242880 | tf_op jit(solution)/shard_map/dot_general | solution.py:123
  162.9 82.1 %reduce-scatter.2.cloned.1.call-done = bf16[128,512]{1,0:T(8,128)(2,1)} async-done(((bf16[2048,512]{1,0:T(8,128)(2,1)}), bf16[128,512]{1,0:T(8,128)(2,1)}) %reduce-scatter.2.cloned.1.call-update) | async-done | bytes 131088 | tf_op jit(solution)/shard_map/reduce_scatter | solution.py:134
  245.0 149.0 %all-reduce.1 = f32[128,512]{1,0:T(8,128)} all-reduce(bf16[128,512]{1,0:T(8,128)(2,1)} %reduce-scatter.2.cloned.1.call-done), channel_id=1, replica_groups=mesh['dp'=32,'point'=16] {'dp'}, use_global_device_ids=true, to_apply=%region_13.14 | all-reduce | flops 65536 | bytes 393216 | tf_op jit(solution)/shard_map/psum | solution.py:142
  (35 shorter events, 0.2 us)
Async XLA Ops:
  7.2 93.2 %copy-start = (bf16[512,1536]{1,0:T(8,128)(2,1)S(1)}, bf16[512,1536]{1,0:T(8,128)(2,1)}, u32[]{:S(2)}) copy-start(bf16[512,1536]{1,0:T(8,128)(2,1)} %param.11) | copy-start | bytes 4718596
  7.2 35.2 %copy-start.2 = (bf16[1,2,256,512]{3,2,1,0:T(8,128)(2,1)S(1)}, bf16[1,2,256,512]{3,2,1,0:T(8,128)(2,1)}, u32[]{:S(2)}) copy-start(bf16[1,2,256,512]{3,2,1,0:T(8,128)(2,1)} %param.8) | copy-start | bytes 1572868
  7.2 139.5 %all-gather.3.cloned.1.call-start = ((), (), s32[]{:S(2)}) async-start(), calls=%async_computation.3 | async-start | bytes 2228224 | tf_op jit(solution)/shard_map/all_gather | solution.py:118
  36.8 33.8 %all-to-all-start = ((s32[2,16,32]{2,0,1:T(2,128)}), s32[2,16,32]{2,0,1:T(2,128)S(1)}, u32[]{:S(2)}, u32[]{:S(2)}) async-start(s32[2,16,32]{2,0,1:T(2,128)} %copy.26), calls=%async_computation | async-start | bytes 32768 | tf_op jit(solution)/shard_map/all_to_all | solution.py:86
  69.5 7.0 %copy-start.5 = (s32[2]{0:T(128)S(1)}, s32[2]{0:T(128)}, u32[]{:S(2)}) copy-start(s32[2]{0:T(128)} %constant.64) | copy-start | bytes 28
  69.5 7.1 %copy-start.6 = (s32[2]{0:T(128)S(1)}, s32[2]{0:T(128)}, u32[]{:S(2)}) copy-start(s32[2]{0:T(128)} %constant.67) | copy-start | bytes 28
  70.6 22.3 %all-to-all-start.1 = ((bf16[2,16,32,512]{3,2,0,1:T(8,128)(2,1)}), bf16[2,16,32,512]{3,2,0,1:T(8,128)(2,1)S(1)}, u32[]{:S(2)}, u32[]{:S(2)}) async-start(bf16[2,16,32,512]{3,2,0,1:T(8,128)(2,1)} %copy.28), calls=%async_computation.1 | async-start | bytes 2097152 | tf_op jit(solution)/shard_map/all_to_all | solution.py:79
  76.3 82.3 %all-gather.5.cloned.1.call-start = ((), (), s32[]{:S(2)}) async-start(), calls=%async_computation.4 | async-start | bytes 2228224 | tf_op jit(solution)/shard_map/all_gather | solution.py:125
  100.4 6.0 %copy-start.4 = (s32[1,2,256]{2,1,0:T(2,128)S(1)}, s32[1,2,256]{2,1,0:T(2,128)}, u32[]{:S(2)}) copy-start(s32[1,2,256]{2,1,0:T(2,128)} %param.10) | copy-start | bytes 6148
  101.4 1.2 copy-start.1
  102.5 15.1 %collective-permute-start = (bf16[2,256,1024]{2,1,0:T(8,128)(2,1)S(1)}, bf16[2,256,1024]{2,1,0:T(8,128)(2,1)}, u32[]{:S(2)}, u32[]{:S(2)}) collective-permute-start(bf16[2,256,1024]{2,1,0:T(8,128)(2,1)S(1)} %slice.30), channel_id=1, source_target_pairs={{0,1},{1,2},{2,3},{3,4},{4,5},{5,6},{6,7},{7,8},{8,9},{9,10},{10,1... | collective-permute-start | bytes 3145736 | tf_op jit(solution)/shard_map/ppermute | solution.py:15
  105.1 12.6 %collective-permute-start.1 = (bf16[2,256,1024]{2,1,0:T(8,128)(2,1)S(1)}, bf16[2,256,1024]{2,1,0:T(8,128)(2,1)}, u32[]{:S(2)}, u32[]{:S(2)}) collective-permute-start(bf16[2,256,1024]{2,1,0:T(8,128)(2,1)S(1)} %slice.30), channel_id=1, source_target_pairs={{1,0},{2,1},{3,2},{4,3},{5,4},{6,5},{7,6},{8,7},{9,8},{10,9},{11,1... | collective-permute-start | bytes 3145736 | tf_op jit(solution)/shard_map/ppermute | solution.py:18
  106.4 4.4 %collective-permute-start.2 = (s32[2,256]{1,0:T(2,128)S(1)}, s32[2,256]{1,0:T(2,128)S(1)}, u32[]{:S(2)}, u32[]{:S(2)}) collective-permute-start(s32[2,256]{1,0:T(2,128)S(1)} %add_bitcast_fusion.1), channel_id=1, source_target_pairs={{0,1},{1,2},{2,3},{3,4},{4,5},{5,6},{6,7},{7,8},{8,9},{9,10},{10,1... | collective-permute-start | bytes 6152 | tf_op jit(solution)/shard_map/ppermute | solution.py:15
  109.4 4.0 collective-permute-start.3
  110.7 134.3 %reduce-scatter.2.cloned.1.call-start = ((), (), s32[]{:S(2)}) async-start(), calls=%async_computation.5 | async-start | bytes 2228224 | tf_op jit(solution)/shard_map/reduce_scatter | solution.py:134
  121.2 5.3 %copy-start.3 = (bf16[2,256,512]{1,2,0:T(8,128)(2,1)S(1)}, bf16[2,256,512]{1,2,0:T(8,128)(2,1)}, u32[]{:S(2)}) copy-start(bf16[2,256,512]{1,2,0:T(8,128)(2,1)} %copy.31) | copy-start | bytes 1572868
  137.8 7.9 %copy-start.7 = (bf16[512,512]{1,0:T(8,128)(2,1)S(1)}, bf16[512,512]{1,0:T(8,128)(2,1)}, u32[]{:S(2)}) copy-start(bf16[512,512]{1,0:T(8,128)(2,1)} %param.12) | copy-start | bytes 1572868
  146.6 5.0 %copy-start.8 = (bf16[1,2,256,512]{3,2,1,0:T(8,128)(2,1)S(1)}, bf16[1,2,256,512]{3,2,1,0:T(8,128)(2,1)}, u32[]{:S(2)}) copy-start(bf16[1,2,256,512]{3,2,1,0:T(8,128)(2,1)} %param.15) | copy-start | bytes 1572868
  150.2 1.4 copy-start.9
Sparse Core Ops, SparseCore 0:
  10.2 45.7 all-gather.2
  110.8 47.7 all-gather.4
  161.5 83.4 reduce-scatter.1
where the time goes:
time: 401 us; the launch traced here: 400 us
  blocking collectives  149 us (37%)
  waiting for transfers between devices  106 us (26%)
  local copies, waits for them, and re-layouts  75.4 us (19%)
  matrix products  30.6 us (8%)
  starting transfers between devices  19.5 us (5%)
  between operations  14.1 us (4%)
  other arithmetic  5.86 us (1%)
    psum x1, blocking collectives, on_device(): grad_down = lax.psum(grad_part, 'dp')  149 us
    reduce_scatter x1, waiting for transfers between devices, on_device(): lax.psum_scatter(lax.dot_general(hidden, cot_rows, (((0,), (0,)), ((), ()...  82.1 us
    scatter x1, local copies, waits for them, and re-layouts, fill_send(): jnp.zeros((capacity, features.shape[1]), features.dtype).at[where_to]  27.1 us
    scatter x1, local copies, waits for them, and re-layouts, fill_labels(): return jnp.full((capacity,), empty_mark, jnp.int32).at[where_to].set(labels)  24.5 us
    all_to_all x1, waiting for transfers between devices, on_device(): lax.all_to_all(outgoing.reshape(clouds, devices, capacity, width), 'point...  16.2 us
    sub x1, matrix products, attend(): weights = jnp.where(allowed, jnp.exp(scores - peak), 0.0)  11.4 us
  transfers between devices with their start and end apart: 9, of which 4 were waited for; matrix products, arithmetic and copies ran while one was open for 27% of the time, Pallas kernels for 0%

commit v1 on v0

v1 whole, which is shorter than its diff:
```python
import math

import jax
import jax.numpy as jnp
from jax import lax
from jax.experimental import pallas as pl
from jax.experimental.pallas import tpu as pltpu
from jax.sharding import PartitionSpec as P

HEADS = 8
LANES = 128
TAG_ROWS = 16
LOG2E = math.log2(math.e)
PARAMS = pltpu.CompilerParams(vmem_limit_bytes=48 * 1024 * 1024)
F32 = jnp.float32
BF16 = jnp.bfloat16


def dot(a, b, dims=((1,), (0,))):
    return lax.dot_general(a, b, (dims, ((), ())), preferred_element_type=F32)


def normalize(wide):
    centre = jnp.mean(wide, axis=-1, keepdims=True)
    spread = jnp.mean(jnp.square(wide - centre), axis=-1, keepdims=True)
    return ((wide - centre) * lax.rsqrt(spread + 1e-05)).astype(BF16)


def column(row):
    return jnp.transpose(jnp.broadcast_to(row, (LANES, row.shape[1])))


def dispatch_kernel(ranks_ref, points_ref, out_ref):
    clouds, length, width = points_ref.shape
    devices, _, capacity, _ = out_ref.shape
    ranks = ranks_ref[...]
    target = ranks // length
    local = ranks - target * length
    before = (
        lax.broadcasted_iota(jnp.int32, (length, length), 0)
        < lax.broadcasted_iota(jnp.int32, (length, length), 1)
    ).astype(F32).astype(BF16)
    for c in range(clouds):
        goes = lax.broadcasted_iota(jnp.int32, (devices, length), 0) == target[c : c + 1]
        ones = goes.astype(F32)
        earlier = dot(ones.astype(BF16), before)
        slot = jnp.sum(earlier * ones, axis=0, keepdims=True).astype(jnp.int32)
        where_to = target[c : c + 1] * capacity + slot
        pick = (
            lax.broadcasted_iota(jnp.int32, (devices * capacity, length), 0) == where_to
        ).astype(F32).astype(BF16)
        places = column((local[c : c + 1] + 1).astype(F32)).astype(BF16)
        rows = dot(pick, points_ref[c]).astype(BF16)
        marks = dot(pick, places).astype(BF16)
        out_ref[:, c, :, :width] = rows.reshape(devices, capacity, width)
        out_ref[:, c, :, width:] = marks.reshape(devices, capacity, LANES)


def project_kernel(arrived_ref, tags_ref, w_ref, ordered_ref, halo_ref, qkv_ref):
    devices, clouds, capacity, _ = arrived_ref.shape
    _, length, width = ordered_ref.shape
    slots = devices * capacity
    for c in range(clouds):
        rows = arrived_ref[:, c, :, :width].reshape(slots, width)
        marks = arrived_ref[:, c, :, width:].reshape(slots, LANES).astype(F32)
        wide_marks = jnp.concatenate([marks] * (length // LANES), axis=1)
        here = lax.broadcasted_iota(jnp.int32, (slots, length), 1).astype(F32) + 1.0
        put = (wide_marks == here).astype(F32).astype(BF16)
        ordered = dot(put, rows, ((0,), (0,)))
        ordered_ref[c] = ordered.astype(BF16)
        normed = normalize(ordered)
        halo_ref[c, :length] = normed
        tag_row = jnp.concatenate(
            [tags_ref[c : c + 1].astype(F32) + 1.0, jnp.zeros((1, width - length), F32)], axis=1
        )
        halo_ref[c, length:] = jnp.broadcast_to(tag_row, (TAG_ROWS, width)).astype(BF16)
        qkv_ref[c] = dot(normed, w_ref[...]).astype(BF16)


def attend_kernel(qkv_ref, low_ref, high_ref, halo_ref, ordered_ref, w_ref, w_out_ref, res_ref, normed_ref):
    clouds, length, width = ordered_ref.shape
    head = width // HEADS
    pair = LANES // head
    first = lax.broadcasted_iota(jnp.int32, (length, LANES), 1) < head
    ones = jnp.ones((length, LANES), BF16)
    scale = head ** (-0.5) * LOG2E
    for c in range(clouds):
        own_tags = halo_ref[c, length : length + TAG_ROWS, :length].astype(F32)[:1]
        asks = column(own_tags)
        asks = jnp.concatenate([asks] * (length // LANES), axis=1)
        sides = []
        for ref in (low_ref, high_ref):
            kv = dot(ref[c, :length], w_ref[:, width:]).astype(BF16)
            sides.append((kv, ref[c, length : length + TAG_ROWS, :length].astype(F32)[:1]))
        sides.append((qkv_ref[c, :, width:], own_tags))
        allowed = [asks == tags for _, tags in sides]
        for h in range(HEADS // pair):
            lanes = slice(h * LANES, (h + 1) * LANES)
            values = slice(width + h * LANES, width + (h + 1) * LANES)
            queries = qkv_ref[c, :, lanes]
            mixed = []
            for inside in (first, ~first):
                asked = jnp.where(inside, queries, jnp.zeros_like(queries))
                scores = [
                    jnp.where(ok, dot(asked, kv[:, lanes], ((1,), (1,))), -1e30)
                    for (kv, _), ok in zip(sides, allowed)
                ]
                peak = jnp.max(
                    jnp.maximum(jnp.maximum(scores[0], scores[1]), scores[2]), axis=1, keepdims=True
                )
                total = None
                for (kv, _), s in zip(sides, scores):
                    weights = jnp.exp2((s - peak) * scale).astype(BF16)
                    part = dot(weights, jnp.concatenate([kv[:, values], ones], axis=1))
                    total = part if total is None else total + part
                mixed.append(total[:, :LANES] / total[:, LANES:])
            attended = jnp.where(first, mixed[0], mixed[1]).astype(BF16)
            part = dot(attended, w_out_ref[lanes, :])
            out = part if h == 0 else out + part
        residual = (ordered_ref[c].astype(F32) + out).astype(BF16)
        rows = slice(c * length, (c + 1) * length)
        res_ref[rows] = residual
        normed_ref[rows] = normalize(residual.astype(F32))


def up_kernel(parity_ref, normed_ref, w_up_ref, cot_ref, hidden_ref, grad_ref):
    blocks, _, units, _ = w_up_ref.shape
    parity = parity_ref[0]
    half = units // 2
    for j in range(0, blocks, 2):
        weights = w_up_ref[j : j + 2, parity].reshape(2 * units, -1)
        product = dot(weights, normed_ref[...], ((1,), (1,)))
        hidden = jax.nn.gelu(product).astype(BF16)
        hidden_ref[j * units : (j + 2) * units] = hidden
        grad = dot(hidden, cot_ref[...]).astype(BF16)
        for k in range(2):
            grad_ref[0, j + k] = grad[k * units : k * units + half]
            grad_ref[1, j + k] = grad[k * units + half : (k + 1) * units]


def down_kernel(parity_ref, res_ref, one_ref, two_ref, w_down_ref, out_ref):
    blocks, _, units, width = w_down_ref.shape
    parity = parity_ref[0]
    total = dot(one_ref[...], w_down_ref[:, parity].reshape(blocks * units, width), ((0,), (0,)))
    total += dot(two_ref[...], w_down_ref[:, 1 - parity].reshape(blocks * units, width), ((0,), (0,)))
    out_ref[...] = (res_ref[...].astype(F32) + total).astype(BF16)


VMEM = pl.BlockSpec(memory_space=pltpu.VMEM)
SMEM = pl.BlockSpec(memory_space=pltpu.SMEM)


def call(kernel, outs, args, scalars=0, flops=0):
    return pl.pallas_call(
        kernel,
        out_shape=[jax.ShapeDtypeStruct(shape, BF16) for shape in outs],
        in_specs=[SMEM] * scalars + [VMEM] * (len(args) - scalars),
        out_specs=[VMEM] * len(outs),
        compiler_params=PARAMS,
        cost_estimate=pl.CostEstimate(
            flops=flops, bytes_accessed=sum(2 * math.prod(s) for s in outs) * 2, transcendentals=0
        ),
    )(*args)


def on_device(points, hilbert_rank, patch_id, w_qkv, w_out, w_up, w_down, cotangent):
    clouds, length, width = points.shape[1:]
    rows_all = clouds * length
    devices = lax.axis_size("point")
    groups = lax.axis_size("dp")
    units = w_up.shape[0]
    capacity = 2 * length // devices
    me = lax.axis_index("point")
    parity = (me & 1).reshape(1).astype(jnp.int32)
    up_all = lax.all_gather(w_up, "point", axis=0, tiled=True)
    down_all = lax.all_gather(w_down, "point", axis=0, tiled=True)

    (outgoing,) = call(
        dispatch_kernel,
        [(devices, clouds, capacity, width + LANES)],
        (hilbert_rank[0], points[0]),
        flops=4 * rows_all * devices * capacity * width // clouds,
    )
    arrived = lax.all_to_all(outgoing, "point", 0, 0, tiled=True)
    ordered, halo, qkv = call(
        project_kernel,
        [(clouds, length, width), (clouds, length + TAG_ROWS, width), (clouds, length, 3 * width)],
        (arrived, patch_id[0], w_qkv),
        flops=2 * rows_all * width * 4 * width,
    )
    forward = [(i, i + 1) for i in range(devices - 1)]
    backward = [(i + 1, i) for i in range(devices - 1)]
    low = lax.ppermute(halo, "point", forward)
    high = lax.ppermute(halo, "point", backward)
    residual, normed_two = call(
        attend_kernel,
        [(rows_all, width), (rows_all, width)],
        (qkv, low, high, halo, ordered, w_qkv, w_out),
        flops=2 * rows_all * width * (4 * width + 12 * length),
    )

    blocks = devices // 2
    halves = [(blocks * units, rows_all), (2, blocks, units // 2, width)]
    up_blocks = up_all.reshape(blocks, 2, units, width)
    cot_rows = cotangent[0].reshape(rows_all, width)
    up_flops = 4 * rows_all * width * units * blocks
    hidden_two, grad_two = call(
        up_kernel, halves, (1 - parity, normed_two, up_blocks, cot_rows), 1, up_flops
    )
    grad_got = lax.ppermute(grad_two, "point", [(i, i ^ 1) for i in range(devices)])
    hidden_one, grad_one = call(
        up_kernel, halves, (parity, normed_two, up_blocks, cot_rows), 1, up_flops
    )
    grad = (grad_one.astype(F32) + grad_got.astype(F32)).astype(BF16)
    grad = grad.reshape(2 * blocks, units // 2, width)

    stages = groups // 2
    planes = [
        [(z * 2 + h) * devices + j * 2 + core for h in range(2) for j in range(blocks)]
        for z in range(stages)
        for core in range(2)
    ]
    grad = lax.all_to_all(
        grad, ("dp", "point"), 0, 0, axis_index_groups=planes, tiled=True
    )
    grad = jnp.sum(grad.astype(F32), axis=0).astype(BF16)
    piece = units // groups
    grad = lax.all_to_all(
        grad.reshape(stages, piece, width),
        "dp",
        0,
        0,
        axis_index_groups=[[z * 2 + h for z in range(stages)] for h in range(2)],
        tiled=True,
    )
    grad = jnp.sum(grad.astype(F32), axis=0).astype(BF16)
    grad = lax.all_to_all(
        jnp.broadcast_to(grad[None], (groups, piece, width)), "dp", 0, 0, tiled=True
    )
    grad = grad.reshape(stages, 2, piece, width).transpose(1, 0, 2, 3).reshape(units, width)
    grad_down = grad.astype(F32)

    (layer_out,) = call(
        down_kernel,
        [(rows_all, width)],
        (parity, residual, hidden_one, hidden_two, down_all.reshape(blocks, 2, units, width)),
        1,
        2 * rows_all * width * devices * units,
    )
    return layer_out.reshape(1, clouds, length, width), grad_down


def solution(mesh):
    placed = (
        P("dp", None, "point", None),
        P("dp", None, "point"),
        P("dp", None, "point"),
        P(),
        P(),
        P("point", None),
        P("point", None),
        P("dp", None, "point", None),
    )
    return jax.shard_map(
        on_device,
        mesh=mesh,
        in_specs=placed,
        out_specs=(P("dp", None, "point", None), P("point", None)),
        check_vma=False,
    )
```

time: 401 us -> 169 us (0.42)
  the two profiles are of different devices: /device:TPU:32 before, /device:TPU:2 now
where the time goes in v1:
time: 169 us; the launch traced here: 168 us
  blocking collectives  50.6 us (30%)
  waiting for transfers between devices  45.9 us (27%)
  starting transfers between devices  21.3 us (13%)
  Pallas kernels  19.5 us (12%)
  local copies, waits for them, and re-layouts  14.8 us (9%)
  between operations  14.2 us (8%)
  other arithmetic  1.78 us (1%)
    all_to_all x1, blocking collectives, on_device(): lax.all_to_all(grad.reshape(stages, piece, width), 'dp', 0, 0, axis_index...  25.3 us
    all_to_all x1, blocking collectives, on_device(): lax.all_to_all(grad, ('dp', 'point'), 0, 0, axis_index_groups=planes, til...  25.3 us
    all_to_all x1, waiting for transfers between devices, on_device(): arrived = lax.all_to_all(outgoing, 'point', 0, 0, tiled=True)  19.6 us
    pallas_call x6, Pallas kernels, call(): pl.pallas_call(kernel, out_shape=[jax.ShapeDtypeStruct(shape, BF16) for s...  19.5 us
    unnamed x32, local copies, waits for them, and re-layouts  13.2 us
    all_to_all x1, waiting for transfers between devices, on_device(): lax.all_to_all(jnp.broadcast_to(grad[None], (groups, piece, width)), 'dp'...  12.4 us
    all_to_all x1, starting transfers between devices, on_device(): arrived = lax.all_to_all(outgoing, 'point', 0, 0, tiled=True)  9.4 us
    ppermute x1, waiting for transfers between devices, on_device(): low = lax.ppermute(halo, 'point', forward)  8.25 us
  transfers between devices with their start and end apart: 7, of which 4 were waited for; matrix products, arithmetic and copies ran while one was open for 1% of the time, Pallas kernels for 12%

profile of v1, /device:TPU:2, one launch (start us, length us, event | category | flops | bytes accessed | tf_op | source)
XLA Modules:
  0.0 168.1 jit_solution(2154212031431514811)
XLA Ops:
  7.2 0.0 all-gather.3.cloned.1.call-start
  7.2 0.7 all-gather.3.cloned.1.call-update
  7.9 0.0 copy-start.1
  7.9 1.0 copy-done.1
  8.9 0.0 copy-start.2
  8.9 0.7 copy-done.2
  9.6 0.0 copy-start.5
  9.6 0.0 copy-start.9
  9.6 1.9 %shard_map.95 = bf16[16,2,32,640]{3,2,1,0:T(8,128)(2,1)} custom-call(s32[2,256]{1,0:T(2,128)S(1)} %bitcast.15, bf16[2,256,512]{2,1,0:T(8,128)(2,1)S(1)} %bitcast.14), custom_call_target="tpu_custom_call" | custom-call | flops 268435456 | bytes 2621440 | tf_op jit(solution)/shard_map/pallas_call | solution.py:154
  11.6 9.4 %all-to-all-start = ((bf16[16,2,32,640]{3,2,1,0:T(8,128)(2,1)}), bf16[16,2,32,640]{3,2,1,0:T(8,128)(2,1)S(1)}, u32[]{:S(2)}, u32[]{:S(2)}) async-start(bf16[16,2,32,640]{3,2,1,0:T(8,128)(2,1)} %shard_map.95), calls=%async_computation | async-start | bytes 2621440 | tf_op jit(solution)/shard_map/all_to_all | solution.py:184
  21.0 0.0 all-gather.5.cloned.1.call-start
  21.0 0.7 all-gather.5.cloned.1.call-update
  21.7 19.6 %all-to-all-done.arrived_ref = bf16[16,2,32,640]{3,2,1,0:T(8,128)(2,1)S(1)} async-done(((bf16[16,2,32,640]{3,2,1,0:T(8,128)(2,1)}), bf16[16,2,32,640]{3,2,1,0:T(8,128)(2,1)S(1)}, u32[]{:S(2)}, u32[]{:S(2)}) %all-to-all-start) | async-done | bytes 1310752 | tf_op jit(solution)/shard_map/all_to_all | solution.py:184
  41.3 0.0 copy-done.5
  41.3 0.0 copy-done.9
  41.3 1.9 %shard_map.96 = (bf16[2,256,512]{2,1,0:T(8,128)(2,1)S(1)}, bf16[2,272,512]{2,1,0:T(8,128)(2,1)S(1)}, bf16[2,256,1536]{2,1,0:T(8,128)(2,1)S(1)}) custom-call(bf16[16,2,32,640]{3,2,1,0:T(8,128)(2,1)S(1)} %all-to-all-done.arrived_ref, s32[2,256]{1,0:T(2,128)S(1)} %bitcast.20, bf16[512,1536]{1,0:T(8,128)(2,1)S(1)} %copy-done.5), custom_call_target="tpu_custom_call" | custom-call | flops 1073741824 | bytes 5308416 | tf_op jit(solution)/shard_map/pallas_call | solution.py:154
  43.2 0.0 copy-start.10
  43.2 1.2 copy-done.10
  44.4 0.0 copy-start.14
  44.4 0.8 copy-done.14
  45.2 2.0 %collective-permute-start = (bf16[2,272,512]{2,1,0:T(8,128)(2,1)S(1)}, bf16[2,272,512]{2,1,0:T(8,128)(2,1)S(1)}, u32[]{:S(2)}, u32[]{:S(2)}) collective-permute-start(bf16[2,272,512]{2,1,0:T(8,128)(2,1)S(1)} %get-tuple-element.12.halo_ref), channel_id=1, source_target_pairs={{0,1},{1,2},{2,3},{3,4},{4,5},{5,6},{6,7},{7,8},{8,9},{9,10},{10,1... | collective-permute-start | bytes 1671176 | tf_op jit(solution)/shard_map/ppermute | solution.py:193
  47.2 3.5 %collective-permute-start.1 = (bf16[2,272,512]{2,1,0:T(8,128)(2,1)S(1)}, bf16[2,272,512]{2,1,0:T(8,128)(2,1)S(1)}, u32[]{:S(2)}, u32[]{:S(2)}) collective-permute-start(bf16[2,272,512]{2,1,0:T(8,128)(2,1)S(1)} %get-tuple-element.12.halo_ref), channel_id=1, source_target_pairs={{1,0},{2,1},{3,2},{4,3},{5,4},{6,5},{7,6},{8,7},{9,8},{10,9},{11,1... | collective-permute-start | bytes 1671176 | tf_op jit(solution)/shard_map/ppermute | solution.py:194
  50.8 8.3 %collective-permute-done.low_ref = bf16[2,272,512]{2,1,0:T(8,128)(2,1)S(1)} collective-permute-done((bf16[2,272,512]{2,1,0:T(8,128)(2,1)S(1)}, bf16[2,272,512]{2,1,0:T(8,128)(2,1)S(1)}, u32[]{:S(2)}, u32[]{:S(2)}) %collective-permute-start) | collective-permute-done | bytes 557088 | tf_op jit(solution)/shard_map/ppermute | solution.py:193
  59.0 4.3 %collective-permute-done.1.high_ref = bf16[2,272,512]{2,1,0:T(8,128)(2,1)S(1)} collective-permute-done((bf16[2,272,512]{2,1,0:T(8,128)(2,1)S(1)}, bf16[2,272,512]{2,1,0:T(8,128)(2,1)S(1)}, u32[]{:S(2)}, u32[]{:S(2)}) %collective-permute-start.1) | collective-permute-done | bytes 557088 | tf_op jit(solution)/shard_map/ppermute | solution.py:194
  63.3 0.0 copy-start.6
  63.3 1.0 copy-done.6
  64.3 0.0 copy-start.11
  64.3 1.4 copy-done.11
  65.7 0.0 copy-start.15
  65.7 1.0 copy-done.15
  66.8 0.0 copy-start.7
  66.8 9.9 %shard_map.97 = (bf16[512,512]{1,0:T(8,128)(2,1)S(1)}, bf16[512,512]{1,0:T(8,128)(2,1)S(1)}) custom-call(bf16[2,256,1536]{2,1,0:T(8,128)(2,1)S(1)} %copy-done.11, bf16[2,272,512]{2,1,0:T(8,128)(2,1)S(1)} %collective-permute-done.low_ref, bf16[2,272,512]{2,1,0:T(8,128)(2,1)S(1)} %collective-permute-done.1.high_ref, ...), custom_call_target="tpu_custom_call" | custom-call | flops 2684354560 | bytes 2097152 | tf_op jit(solution)/shard_map/pallas_call | solution.py:154
  76.7 0.0 copy-start.12
  76.7 0.8 copy-done.12
  77.5 0.0 all-gather.3.cloned.1.call-done
  77.5 0.0 copy-done.7
  77.5 0.0 copy-start.3
  77.5 1.6 copy-done.3
  79.1 0.0 copy-start.13
  79.1 1.0 copy-done.13
  80.1 0.0 copy-start.4
  80.1 1.9 %shard_map.99 = (bf16[1024,512]{1,0:T(8,128)(2,1)S(1)}, bf16[2,8,64,512]{3,2,1,0:T(8,128)(2,1)S(1)}) custom-call(s32[1]{0:T(128)S(6)} %sub.3.parity_ref, bf16[512,512]{1,0:T(8,128)(2,1)S(1)} %copy-done.13, bf16[8,2,128,512]{3,2,1,0:T(8,128)(2,1)S(1)} %bitcast.16, bf16[512,512]{1,0:T(8,128)(2,1)S(1)} %bitcast.18), custom_call_target="tpu_custom_call" | custom-call | flops 1073741824 | bytes 4194304 | tf_op jit(solution)/shard_map/pallas_call | solution.py:154
  82.0 2.1 %collective-permute-start.2 = (bf16[2,8,64,512]{3,2,1,0:T(8,128)(2,1)S(1)}, bf16[2,8,64,512]{3,2,1,0:T(8,128)(2,1)S(1)}, u32[]{:S(2)}, u32[]{:S(2)}) collective-permute-start(bf16[2,8,64,512]{3,2,1,0:T(8,128)(2,1)S(1)} %get-tuple-element.19), channel_id=1, source_target_pairs={{0,1},{1,0},{2,3},{3,2},{4,5},{5,4},{6,7},{7,6},{8,9},{9,8},{10,11... | collective-permute-start | bytes 3145736 | tf_op jit(solution)/shard_map/ppermute | solution.py:210
  84.1 0.0 copy-done.4
  84.1 0.0 copy-start.8
  84.1 1.0 copy-done.8
  85.2 1.9 %shard_map.98 = (bf16[1024,512]{1,0:T(8,128)(2,1)S(1)}, bf16[2,8,64,512]{3,2,1,0:T(8,128)(2,1)S(1)}) custom-call(s32[1]{0:T(128)} %bitcast.parity_ref, bf16[512,512]{1,0:T(8,128)(2,1)S(1)} %copy-done.13, bf16[8,2,128,512]{3,2,1,0:T(8,128)(2,1)S(1)} %bitcast.17, bf16[512,512]{1,0:T(8,128)(2,1)S(1)} %bitcast.19), custom_call_target="tpu_custom_call" | custom-call | flops 1073741824 | bytes 4194304 | tf_op jit(solution)/shard_map/pallas_call | solution.py:154
  87.1 0.0 collective-permute-done.2
  87.1 0.3 add_convert_fusion
  87.4 25.3 %all_to_all.20 = bf16[16,64,512]{2,1,0:T(8,128)(2,1)} all-to-all(bf16[16,64,512]{2,1,0:T(8,128)(2,1)S(1)} %bitcast.21), channel_id=1, replica_groups={{0,2,4,6,8,10,12,14,16,18,20,22,24,26,28,30},{1,3,5,7,9,11,13,15,17,19,..., dimensions={0} | all-to-all | bytes 2097152 | tf_op jit(solution)/shard_map/all_to_all | solution.py:223
  112.7 1.4 reduce_sum.24
  114.1 25.3 %all_to_all.21 = bf16[16,4,512]{2,1,0:T(4,128)(2,1)S(1)} all-to-all(bf16[16,4,512]{2,1,0:T(4,128)(2,1)S(1)} %reshape.34), channel_id=1, replica_groups={{0,32,64,96,128,160,192,224,256,288,320,352,384,416,448,480},{16,48,80,..., dimensions={0} | all-to-all | bytes 131072 | tf_op jit(solution)/shard_map/all_to_all | solution.py:228
  139.5 0.7 broadcast_in_dim.2
  140.2 4.2 %all-to-all-start.3 = ((bf16[32,4,512]{2,1,0:T(4,128)(2,1)}), bf16[32,4,512]{2,1,0:T(4,128)(2,1)S(1)}, u32[]{:S(2)}, u32[]{:S(2)}) async-start(bf16[32,4,512]{2,1,0:T(4,128)(2,1)} %broadcast_in_dim.2), calls=%async_computation.3 | async-start | bytes 262144 | tf_op jit(solution)/shard_map/all_to_all | solution.py:237
  144.4 0.0 all-gather.5.cloned.1.call-done
  144.4 0.0 copy-start
  144.4 1.6 copy-done
  146.0 2.1 %shard_map.100 = bf16[512,512]{1,0:T(8,128)(2,1)} custom-call(s32[1]{0:T(128)} %bitcast.parity_ref, bf16[512,512]{1,0:T(8,128)(2,1)S(1)} %get-tuple-element.14.res_ref, bf16[1024,512]{1,0:T(8,128)(2,1)S(1)} %get-tuple-element.16.one_ref, bf16[1024,512]{1,0:T(8,128)(2,1)S(1)} %get-tuple-element.17.two_ref, bf16[8,2,128,512]{3,2,1,0:T(8,128)(2,1)S(1)} %bitcast.13), custom_call_target="tpu_custom_call" | custom-call | flops 1073741824 | bytes 1048576 | tf_op jit(solution)/shard_map/pallas_call | solution.py:154
  148.1 12.4 %all-to-all-done.3 = bf16[32,4,512]{2,1,0:T(4,128)(2,1)S(1)} async-done(((bf16[32,4,512]{2,1,0:T(4,128)(2,1)}), bf16[32,4,512]{2,1,0:T(4,128)(2,1)S(1)}, u32[]{:S(2)}, u32[]{:S(2)}) %all-to-all-start.3) | async-done | bytes 131104 | tf_op jit(solution)/shard_map/all_to_all | solution.py:237
  160.5 0.8 reshape.35
  (4 shorter events, 0.1 us)
Async XLA Ops:
  7.2 70.3 %all-gather.3.cloned.1.call-start = ((), (), s32[]{:S(2)}) async-start(), calls=%async_computation.4 | async-start | bytes 2228224 | tf_op jit(solution)/shard_map/all_gather | solution.py:175
  7.9 1.0 copy-start.1
  8.9 0.7 copy-start.2
  9.6 31.7 %copy-start.5 = (bf16[512,1536]{1,0:T(8,128)(2,1)S(1)}, bf16[512,1536]{1,0:T(8,128)(2,1)}, u32[]{:S(2)}) copy-start(bf16[512,1536]{1,0:T(8,128)(2,1)} %w_ref.3) | copy-start | bytes 4718596
  9.6 31.7 %copy-start.9 = (s32[1,2,256]{2,1,0:T(2,128)S(1)}, s32[1,2,256]{2,1,0:T(2,128)}, u32[]{:S(2)}) copy-start(s32[1,2,256]{2,1,0:T(2,128)} %param.10) | copy-start | bytes 6148
  11.6 29.8 %all-to-all-start = ((bf16[16,2,32,640]{3,2,1,0:T(8,128)(2,1)}), bf16[16,2,32,640]{3,2,1,0:T(8,128)(2,1)S(1)}, u32[]{:S(2)}, u32[]{:S(2)}) async-start(bf16[16,2,32,640]{3,2,1,0:T(8,128)(2,1)} %shard_map.95), calls=%async_computation | async-start | bytes 2621440 | tf_op jit(solution)/shard_map/all_to_all | solution.py:184
  21.0 123.4 %all-gather.5.cloned.1.call-start = ((), (), s32[]{:S(2)}) async-start(), calls=%async_computation.5 | async-start | bytes 2228224 | tf_op jit(solution)/shard_map/all_gather | solution.py:176
  43.2 1.2 copy-start.10
  44.4 0.8 copy-start.14
  45.2 13.8 %collective-permute-start = (bf16[2,272,512]{2,1,0:T(8,128)(2,1)S(1)}, bf16[2,272,512]{2,1,0:T(8,128)(2,1)S(1)}, u32[]{:S(2)}, u32[]{:S(2)}) collective-permute-start(bf16[2,272,512]{2,1,0:T(8,128)(2,1)S(1)} %get-tuple-element.12.halo_ref), channel_id=1, source_target_pairs={{0,1},{1,2},{2,3},{3,4},{4,5},{5,6},{6,7},{7,8},{8,9},{9,10},{10,1... | collective-permute-start | bytes 1671176 | tf_op jit(solution)/shard_map/ppermute | solution.py:193
  47.2 16.1 %collective-permute-start.1 = (bf16[2,272,512]{2,1,0:T(8,128)(2,1)S(1)}, bf16[2,272,512]{2,1,0:T(8,128)(2,1)S(1)}, u32[]{:S(2)}, u32[]{:S(2)}) collective-permute-start(bf16[2,272,512]{2,1,0:T(8,128)(2,1)S(1)} %get-tuple-element.12.halo_ref), channel_id=1, source_target_pairs={{1,0},{2,1},{3,2},{4,3},{5,4},{6,5},{7,6},{8,7},{9,8},{10,9},{11,1... | collective-permute-start | bytes 1671176 | tf_op jit(solution)/shard_map/ppermute | solution.py:194
  63.3 1.0 copy-start.6
  64.3 1.4 copy-start.11
  65.7 1.0 copy-start.15
  66.8 10.7 %copy-start.7 = (bf16[1,2,256,512]{3,2,1,0:T(8,128)(2,1)S(1)}, bf16[1,2,256,512]{3,2,1,0:T(8,128)(2,1)}, u32[]{:S(2)}) copy-start(bf16[1,2,256,512]{3,2,1,0:T(8,128)(2,1)} %param.15) | copy-start | bytes 1572868
  76.7 0.8 copy-start.12
  77.5 1.6 copy-start.3
  79.1 1.0 copy-start.13
  80.1 4.0 %copy-start.4 = (bf16[2048,512]{1,0:T(8,128)(2,1)S(1)}, bf16[2048,512]{1,0:T(8,128)(2,1)}, u32[]{:S(2)}) copy-start(bf16[2048,512]{1,0:T(8,128)(2,1)} %all-gather.3.cloned.1.call-done) | copy-start | bytes 6291460
  82.0 5.1 %collective-permute-start.2 = (bf16[2,8,64,512]{3,2,1,0:T(8,128)(2,1)S(1)}, bf16[2,8,64,512]{3,2,1,0:T(8,128)(2,1)S(1)}, u32[]{:S(2)}, u32[]{:S(2)}) collective-permute-start(bf16[2,8,64,512]{3,2,1,0:T(8,128)(2,1)S(1)} %get-tuple-element.19), channel_id=1, source_target_pairs={{0,1},{1,0},{2,3},{3,2},{4,5},{5,4},{6,7},{7,6},{8,9},{9,8},{10,11... | collective-permute-start | bytes 3145736 | tf_op jit(solution)/shard_map/ppermute | solution.py:210
  84.1 1.0 copy-start.8
  140.2 20.3 %all-to-all-start.3 = ((bf16[32,4,512]{2,1,0:T(4,128)(2,1)}), bf16[32,4,512]{2,1,0:T(4,128)(2,1)S(1)}, u32[]{:S(2)}, u32[]{:S(2)}) async-start(bf16[32,4,512]{2,1,0:T(4,128)(2,1)} %broadcast_in_dim.2), calls=%async_computation.3 | async-start | bytes 262144 | tf_op jit(solution)/shard_map/all_to_all | solution.py:237
  144.4 1.6 copy-start
Sparse Core Ops, SparseCore 0:
  10.1 52.4 all-gather.2
  64.7 50.3 all-gather.4

commit v2 on v1

v2 whole, which is shorter than its diff:
```python
import math
from functools import partial

import jax
import jax.numpy as jnp
from jax import lax
from jax.experimental import pallas as pl
from jax.experimental.pallas import tpu as pltpu
from jax.sharding import PartitionSpec as P

HEADS = 8
LANES = 128
TAG_ROWS = 16
LOG2E = math.log2(math.e)
SMALL = 16 * 1024 * 1024
LARGE = 60 * 1024 * 1024
F32 = jnp.float32
BF16 = jnp.bfloat16


def dot(a, b, dims=((1,), (0,))):
    return lax.dot_general(a, b, (dims, ((), ())), preferred_element_type=F32)


def normalize(wide):
    centre = jnp.mean(wide, axis=-1, keepdims=True)
    spread = jnp.mean(jnp.square(wide - centre), axis=-1, keepdims=True)
    return ((wide - centre) * lax.rsqrt(spread + 1e-05)).astype(BF16)


def column(row):
    return jnp.transpose(jnp.broadcast_to(row, (LANES, row.shape[1])))


def dispatch_kernel(ranks_hbm, points_hbm, out_ref, ranks_ref, points_ref, ranks_sem, points_sem):
    clouds, length, width = points_ref.shape
    devices, _, capacity, _ = out_ref.shape
    ranks_copy = pltpu.make_async_copy(ranks_hbm, ranks_ref, ranks_sem)
    ranks_copy.start()
    copies = [
        pltpu.make_async_copy(points_hbm.at[c], points_ref.at[c], points_sem.at[c])
        for c in range(clouds)
    ]
    for copy in copies:
        copy.start()
    before = (
        lax.broadcasted_iota(jnp.int32, (length, length), 0)
        < lax.broadcasted_iota(jnp.int32, (length, length), 1)
    ).astype(F32).astype(BF16)
    ranks_copy.wait()
    ranks = ranks_ref[...]
    target = ranks // length
    local = ranks - target * length
    for c in range(clouds):
        goes = lax.broadcasted_iota(jnp.int32, (devices, length), 0) == target[c : c + 1]
        ones = goes.astype(F32)
        earlier = dot(ones.astype(BF16), before)
        slot = jnp.sum(earlier * ones, axis=0, keepdims=True).astype(jnp.int32)
        where_to = target[c : c + 1] * capacity + slot
        pick = (
            lax.broadcasted_iota(jnp.int32, (devices * capacity, length), 0) == where_to
        ).astype(F32).astype(BF16)
        places = column((local[c : c + 1] + 1).astype(F32)).astype(BF16)
        marks = dot(pick, places).astype(BF16)
        out_ref[:, c, :, width:] = marks.reshape(devices, capacity, LANES)
        copies[c].wait()
        rows = dot(pick, points_ref[c]).astype(BF16)
        out_ref[:, c, :, :width] = rows.reshape(devices, capacity, width)


def place_kernel(arrived_ref, tags_ref, block_ref):
    devices, clouds, capacity, _ = arrived_ref.shape
    length, width = block_ref.shape[1] - TAG_ROWS, block_ref.shape[2]
    slots = devices * capacity
    here = lax.broadcasted_iota(jnp.int32, (slots, length), 1).astype(F32) + 1.0
    for c in range(clouds):
        rows = arrived_ref[:, c, :, :width].reshape(slots, width)
        marks = arrived_ref[:, c, :, width:].reshape(slots, LANES).astype(F32)
        wide_marks = jnp.concatenate([marks] * (length // LANES), axis=1)
        put = (wide_marks == here).astype(F32).astype(BF16)
        block_ref[c, :length] = dot(put, rows, ((0,), (0,))).astype(BF16)
        tag_row = jnp.concatenate(
            [tags_ref[c : c + 1].astype(F32) + 1.0, jnp.zeros((1, width - length), F32)], axis=1
        )
        block_ref[c, length:] = jnp.broadcast_to(tag_row, (TAG_ROWS, width)).astype(BF16)


def tags_of(block, length):
    return block[length:, :length].astype(F32)[:1]


def own_kernel(
    own_ref, w_ref, w_out_ref, cot_ref, query_ref, w_kv_ref, out_copy_ref, cot_copy_ref, mixed_ref, total_ref, peak_ref
):
    clouds, length, width = query_ref.shape
    head = width // HEADS
    first = lax.broadcasted_iota(jnp.int32, (length, LANES), 1) < head
    ones = jnp.ones((length, LANES), BF16)
    scale = head ** (-0.5) * LOG2E
    for c in range(clouds):
        projected = dot(normalize(own_ref[c, :length].astype(F32)), w_ref[...]).astype(BF16)
        query_ref[c] = projected[:, :width]
        tags = tags_of(own_ref[c], length)
        allowed = jnp.concatenate([column(tags)] * (length // LANES), axis=1) == tags
        for h in range(width // LANES):
            lanes = slice(h * LANES, (h + 1) * LANES)
            queries = projected[:, lanes]
            keys = projected[:, width:][:, lanes]
            values = jnp.concatenate([projected[:, 2 * width :][:, lanes], ones], axis=1)
            peaks, sums = [], []
            for inside in (first, ~first):
                asked = jnp.where(inside, queries, jnp.zeros_like(queries))
                scores = jnp.where(allowed, dot(asked, keys, ((1,), (1,))), -1e30)
                peak = jnp.max(scores, axis=1, keepdims=True)
                sums.append(dot(jnp.exp2((scores - peak) * scale).astype(BF16), values))
                peaks.append(peak)
            mixed_ref[c, :, lanes] = jnp.where(first, sums[0][:, :LANES], sums[1][:, :LANES])
            total_ref[c, :, lanes] = jnp.where(first, sums[0][:, LANES:], sums[1][:, LANES:])
            peak_ref[c, :, lanes] = jnp.where(first, peaks[0], peaks[1])
    w_kv_ref[...] = w_ref[:, width:]
    out_copy_ref[...] = w_out_ref[...]
    cot_copy_ref[...] = cot_ref[...]


def halo_kernel(
    own_ref, low_ref, high_ref, query_ref, w_ref, w_out_ref, mixed_ref, total_ref, peak_ref, res_ref, normed_ref
):
    clouds, length, width = query_ref.shape
    head = width // HEADS
    first = lax.broadcasted_iota(jnp.int32, (length, LANES), 1) < head
    ones = jnp.ones((length, LANES), BF16)
    scale = head ** (-0.5) * LOG2E
    for c in range(clouds):
        sides = []
        for ref in (low_ref, high_ref):
            normed = normalize(ref[c, :length].astype(F32))
            sides.append((dot(normed, w_ref[...]).astype(BF16), tags_of(ref[c], length)))
        asks = column(tags_of(own_ref[c], length))
        asks = jnp.concatenate([asks] * (length // LANES), axis=1)
        allowed = [asks == tags for _, tags in sides]
        for h in range(width // LANES):
            lanes = slice(h * LANES, (h + 1) * LANES)
            values = slice(width + h * LANES, width + (h + 1) * LANES)
            queries = query_ref[c, :, lanes]
            old_peak = peak_ref[c, :, lanes]
            peaks, sums = [], []
            for k, inside in enumerate((first, ~first)):
                asked = jnp.where(inside, queries, jnp.zeros_like(queries))
                scores = [
                    jnp.where(ok, dot(asked, kv[:, lanes], ((1,), (1,))), -1e30)
                    for (kv, _), ok in zip(sides, allowed)
                ]
                best = jnp.max(jnp.maximum(scores[0], scores[1]), axis=1, keepdims=True)
                best = jnp.maximum(best, old_peak[:, k * head : k * head + 1])
                part = None
                for (kv, _), s in zip(sides, scores):
                    weights = jnp.exp2((s - best) * scale).astype(BF16)
                    add = dot(weights, jnp.concatenate([kv[:, values], ones], axis=1))
                    part = add if part is None else part + add
                sums.append(part)
                peaks.append(best)
            fade = jnp.exp2((old_peak - jnp.where(first, peaks[0], peaks[1])) * scale)
            above = jnp.where(first, sums[0][:, :LANES], sums[1][:, :LANES])
            under = jnp.where(first, sums[0][:, LANES:], sums[1][:, LANES:])
            above += mixed_ref[c, :, lanes] * fade
            under += total_ref[c, :, lanes] * fade
            part = dot((above / under).astype(BF16), w_out_ref[lanes, :])
            attended = part if h == 0 else attended + part
        residual = (own_ref[c, :length].astype(F32) + attended).astype(BF16)
        rows = slice(c * length, (c + 1) * length)
        res_ref[rows] = residual
        normed_ref[rows] = normalize(residual.astype(F32))


def up_kernel(parity_ref, normed_ref, w_up_ref, cot_ref, hidden_ref, grad_ref):
    blocks, _, units, _ = w_up_ref.shape
    parity = parity_ref[0]
    half = units // 2
    for j in range(0, blocks, 2):
        weights = w_up_ref[j : j + 2, parity].reshape(2 * units, -1)
        product = dot(weights, normed_ref[...], ((1,), (1,)))
        hidden = jax.nn.gelu(product).astype(BF16)
        hidden_ref[j * units : (j + 2) * units] = hidden
        grad = dot(hidden, cot_ref[...]).astype(BF16)
        for k in range(2):
            grad_ref[0, j + k] = grad[k * units : k * units + half]
            grad_ref[1, j + k] = grad[k * units + half : (k + 1) * units]


def down_kernel(parity_ref, res_ref, one_ref, two_ref, w_ref, out_ref):
    blocks, _, units, width = w_ref.shape
    parity = parity_ref[0]
    total = dot(one_ref[...], w_ref[:, parity].reshape(blocks * units, width), ((0,), (0,)))
    total += dot(two_ref[...], w_ref[:, 1 - parity].reshape(blocks * units, width), ((0,), (0,)))
    out_ref[...] = (res_ref[...].astype(F32) + total).astype(BF16)


VMEM = pl.BlockSpec(memory_space=pltpu.VMEM)
SMEM = pl.BlockSpec(memory_space=pltpu.SMEM)
ANY = pl.BlockSpec(memory_space=pl.ANY)


def call(kernel, outs, specs, args, scratch=(), flops=0, out_spec=VMEM, limit=SMALL):
    return pl.pallas_call(
        kernel,
        out_shape=[jax.ShapeDtypeStruct(shape, kind) for shape, kind in outs],
        in_specs=specs,
        out_specs=[out_spec] * len(outs),
        scratch_shapes=list(scratch),
        compiler_params=pltpu.CompilerParams(vmem_limit_bytes=limit),
        cost_estimate=pl.CostEstimate(
            flops=flops, bytes_accessed=sum(4 * math.prod(s) for s, _ in outs), transcendentals=0
        ),
    )(*args)


def on_device(points, hilbert_rank, patch_id, w_qkv, w_out, w_up, w_down, cotangent):
    clouds, length, width = points.shape[1:]
    rows_all = clouds * length
    devices = lax.axis_size("point")
    groups = lax.axis_size("dp")
    units = w_up.shape[0]
    capacity = 2 * length // devices
    me = lax.axis_index("point")
    parity = (me & 1).reshape(1).astype(jnp.int32)
    up_all = lax.all_gather(w_up, "point", axis=0, tiled=True)
    down_all = lax.all_gather(w_down, "point", axis=0, tiled=True)

    forward = [(i, i + 1) for i in range(devices - 1)]
    backward = [(i + 1, i) for i in range(devices - 1)]
    dma = pltpu.SemaphoreType.DMA
    (outgoing,) = call(
        dispatch_kernel,
        [((devices, clouds, capacity, width + LANES), BF16)],
        [ANY, ANY],
        (hilbert_rank[0], points[0]),
        (
            pltpu.VMEM((clouds, length), jnp.int32),
            pltpu.VMEM((clouds, length, width), BF16),
            dma,
            dma((clouds,)),
        ),
        flops=2 * rows_all * devices * capacity * width,
        limit=LARGE,
    )
    arrived = lax.all_to_all(outgoing, "point", 0, 0, tiled=True)
    block = (clouds, length + TAG_ROWS, width)
    (own,) = call(
        place_kernel,
        [(block, BF16)],
        [VMEM, VMEM],
        (arrived, patch_id[0]),
        flops=2 * rows_all * width * devices * capacity,
    )
    low = lax.ppermute(own, "point", forward)
    high = lax.ppermute(own, "point", backward)
    each = (clouds, length, width)
    flat = (rows_all, width)
    query, w_kv, w_out, cot_rows, *sums = call(
        own_kernel,
        [(each, BF16), ((width, 2 * width), BF16), ((width, width), BF16), (flat, BF16)] + [(each, F32)] * 3,
        [VMEM] * 4,
        (own, w_qkv, w_out, cotangent[0].reshape(flat)),
        flops=2 * rows_all * width * (3 * width + 4 * length),
    )

    blocks = devices // 2
    up_blocks = up_all.reshape(blocks, 2, units, width)
    halves = [(blocks * units, rows_all), (2, blocks, units // 2, width)]
    residual, normed_two = call(
        halo_kernel,
        [(flat, BF16), (flat, BF16)],
        [VMEM] * 9,
        (own, low, high, query, w_kv, w_out, *sums),
        flops=2 * rows_all * width * (5 * width + 8 * length),
    )
    up = partial(
        call,
        up_kernel,
        [(shape, BF16) for shape in halves],
        [SMEM] + [VMEM] * 3,
        flops=4 * rows_all * width * units * blocks,
    )
    hidden_two, grad_two = up((1 - parity, normed_two, up_blocks, cot_rows))
    grad_got = lax.ppermute(grad_two, "point", [(i, i ^ 1) for i in range(devices)])
    hidden_one, grad_one = up((parity, normed_two, up_blocks, cot_rows))
    grad = (grad_one.astype(F32) + grad_got.astype(F32)).astype(BF16)
    grad = grad.reshape(2 * blocks, units // 2, width)

    stages = groups // 2
    planes = [
        [(z * 2 + h) * devices + j * 2 + core for h in range(2) for j in range(blocks)]
        for z in range(stages)
        for core in range(2)
    ]
    grad = lax.all_to_all(
        grad, ("dp", "point"), 0, 0, axis_index_groups=planes, tiled=True
    )
    grad = jnp.sum(grad.astype(F32), axis=0).astype(BF16)
    piece = units // groups
    grad = lax.all_to_all(
        grad.reshape(stages, piece, width),
        "dp",
        0,
        0,
        axis_index_groups=[[z * 2 + h for z in range(stages)] for h in range(2)],
        tiled=True,
    )
    grad = jnp.sum(grad.astype(F32), axis=0).astype(BF16)
    grad = lax.all_to_all(
        jnp.broadcast_to(grad[None], (groups, piece, width)), "dp", 0, 0, tiled=True
    )
    grad = grad.reshape(stages, 2, piece, width).transpose(1, 0, 2, 3).reshape(units, width)
    grad_down = grad.astype(F32)

    (layer_out,) = call(
        down_kernel,
        [(flat, BF16)],
        [SMEM] + [VMEM] * 4,
        (parity, residual, hidden_one, hidden_two, down_all.reshape(blocks, 2, units, width)),
        flops=2 * rows_all * width * devices * units,
    )
    return layer_out.reshape(1, clouds, length, width), grad_down


def solution(mesh):
    placed = (
        P("dp", None, "point", None),
        P("dp", None, "point"),
        P("dp", None, "point"),
        P(),
        P(),
        P("point", None),
        P("point", None),
        P("dp", None, "point", None),
    )
    return jax.shard_map(
        on_device,
        mesh=mesh,
        in_specs=placed,
        out_specs=(P("dp", None, "point", None), P("point", None)),
        check_vma=False,
    )
```

time: 169 us -> 161 us (0.953)
  local copies, waits for them, and re-layouts: 14.8 us -> 9.44 us
  waiting for transfers between devices: 45.9 us -> 42.3 us
    unnamed x32 -> x22, local copies, waits for them, and re-layouts: 13.2 us -> 7.91 us
    ppermute x2, waiting for transfers between devices: 12.5 us -> 8.29 us  [the longest x1 4.55 us: on_device(): high = lax.ppermute(own, 'point', backward)]
    pallas_call x6 -> x7, Pallas kernels: 19.5 us -> 20.5 us  [call(): pl.pallas_call(kernel, out_shape=[jax.ShapeDtypeStruct(shape, kind) for s...]
  transfers between devices with their start and end apart: 7 -> 7, of which waited for: 4 -> 5; matrix products, arithmetic and copies ran while one was open for 1% -> 2% of each run, Pallas kernels for 12% -> 13%
where the time goes in v2:
time: 161 us
  blocking collectives  50.8 us (32%)
  waiting for transfers between devices  42.3 us (26%)
  starting transfers between devices  21.4 us (13%)
  Pallas kernels  20.5 us (13%)
  between operations  14.2 us (9%)
  local copies, waits for them, and re-layouts  9.44 us (6%)
  other arithmetic  1.83 us (1%)
    all_to_all x1, blocking collectives, on_device(): lax.all_to_all(grad, ('dp', 'point'), 0, 0, axis_index_groups=planes, til...  25.5 us
    all_to_all x1, blocking collectives, on_device(): lax.all_to_all(grad.reshape(stages, piece, width), 'dp', 0, 0, axis_index...  25.3 us
    pallas_call x7, Pallas kernels, call(): pl.pallas_call(kernel, out_shape=[jax.ShapeDtypeStruct(shape, kind) for s...  20.5 us
    all_to_all x1, waiting for transfers between devices, on_device(): arrived = lax.all_to_all(outgoing, 'point', 0, 0, tiled=True)  19.6 us
    all_to_all x1, waiting for transfers between devices, on_device(): lax.all_to_all(jnp.broadcast_to(grad[None], (groups, piece, width)), 'dp'...  12.4 us
    all_to_all x1, starting transfers between devices, on_device(): arrived = lax.all_to_all(outgoing, 'point', 0, 0, tiled=True)  9.55 us
    unnamed x22, local copies, waits for them, and re-layouts  7.91 us
    ppermute x1, waiting for transfers between devices, on_device(): high = lax.ppermute(own, 'point', backward)  4.55 us
  transfers between devices with their start and end apart: 7, of which 5 were waited for; matrix products, arithmetic and copies ran while one was open for 2% of the time, Pallas kernels for 13%

profile of v2, /device:TPU:2, one launch (start us, length us, event | category | flops | bytes accessed | tf_op | source)
XLA Modules:
  0.0 160.5 jit_solution(4835471490467195814)
XLA Ops:
  7.2 0.0 all-gather.3.cloned.1.call-start
  7.2 0.7 all-gather.3.cloned.1.call-update
  7.9 0.0 copy-start.1
  7.9 3.2 %shard_map.95 = bf16[16,2,32,640]{3,2,1,0:T(8,128)(2,1)} custom-call(s32[2,256]{1,0:T(2,128)} %bitcast.22, bf16[2,256,512]{2,1,0:T(8,128)(2,1)} %bitcast.20), custom_call_target="tpu_custom_call" | custom-call | flops 268435456 | bytes 2621440 | tf_op jit(solution)/shard_map/pallas_call | solution.py:204
  11.1 0.0 copy-start.4
  11.1 9.5 %all-to-all-start = ((bf16[16,2,32,640]{3,2,1,0:T(8,128)(2,1)}), bf16[16,2,32,640]{3,2,1,0:T(8,128)(2,1)S(1)}, u32[]{:S(2)}, u32[]{:S(2)}) async-start(bf16[16,2,32,640]{3,2,1,0:T(8,128)(2,1)} %shard_map.95), calls=%async_computation | async-start | bytes 2621440 | tf_op jit(solution)/shard_map/all_to_all | solution.py:246
  20.7 0.0 all-gather.5.cloned.1.call-start
  20.7 0.7 all-gather.5.cloned.1.call-update
  21.4 19.6 %all-to-all-done.arrived_ref = bf16[16,2,32,640]{3,2,1,0:T(8,128)(2,1)S(1)} async-done(((bf16[16,2,32,640]{3,2,1,0:T(8,128)(2,1)}), bf16[16,2,32,640]{3,2,1,0:T(8,128)(2,1)S(1)}, u32[]{:S(2)}, u32[]{:S(2)}) %all-to-all-start) | async-done | bytes 1310752 | tf_op jit(solution)/shard_map/all_to_all | solution.py:246
  41.0 0.0 copy-done.1
  41.0 0.5 shard_map.96.own_ref
  41.5 2.0 %collective-permute-start = (bf16[2,272,512]{2,1,0:T(8,128)(2,1)S(1)}, bf16[2,272,512]{2,1,0:T(8,128)(2,1)S(1)}, u32[]{:S(2)}, u32[]{:S(2)}) collective-permute-start(bf16[2,272,512]{2,1,0:T(8,128)(2,1)S(1)} %shard_map.96.own_ref), channel_id=1, source_target_pairs={{0,1},{1,2},{2,3},{3,4},{4,5},{5,6},{6,7},{7,8},{8,9},{9,10},{10,1... | collective-permute-start | bytes 1671176 | tf_op jit(solution)/shard_map/ppermute | solution.py:255
  43.6 3.5 %collective-permute-start.1 = (bf16[2,272,512]{2,1,0:T(8,128)(2,1)S(1)}, bf16[2,272,512]{2,1,0:T(8,128)(2,1)S(1)}, u32[]{:S(2)}, u32[]{:S(2)}) collective-permute-start(bf16[2,272,512]{2,1,0:T(8,128)(2,1)S(1)} %shard_map.96.own_ref), channel_id=1, source_target_pairs={{1,0},{2,1},{3,2},{4,3},{5,4},{6,5},{7,6},{8,7},{9,8},{10,9},{11,1... | collective-permute-start | bytes 1671176 | tf_op jit(solution)/shard_map/ppermute | solution.py:256
  47.1 0.0 copy-done.4
  47.1 0.0 copy-start.5
  47.1 1.0 copy-done.5
  48.2 0.0 copy-start.6
  48.2 1.0 copy-done.6
  49.2 3.0 %shard_map.97 = (bf16[2,256,512]{2,1,0:T(8,128)(2,1)S(1)}, bf16[512,1024]{1,0:T(8,128)(2,1)S(1)}, bf16[512,512]{1,0:T(8,128)(2,1)S(1)}, bf16[512,512]{1,0:T(8,12...) custom-call(bf16[2,272,512]{2,1,0:T(8,128)(2,1)S(1)} %shard_map.96.own_ref, ...), custom_call_target="tpu_custom_call" | custom-call | flops 1342177280 | bytes 8388608 | tf_op jit(solution)/shard_map/pallas_call | solution.py:204
  52.2 0.0 copy-start.7
  52.2 0.8 copy-done.7
  53.0 3.7 %collective-permute-done.low_ref = bf16[2,272,512]{2,1,0:T(8,128)(2,1)S(1)} collective-permute-done((bf16[2,272,512]{2,1,0:T(8,128)(2,1)S(1)}, bf16[2,272,512]{2,1,0:T(8,128)(2,1)S(1)}, u32[]{:S(2)}, u32[]{:S(2)}) %collective-permute-start) | collective-permute-done | bytes 557088 | tf_op jit(solution)/shard_map/ppermute | solution.py:255
  56.8 4.6 %collective-permute-done.1.high_ref = bf16[2,272,512]{2,1,0:T(8,128)(2,1)S(1)} collective-permute-done((bf16[2,272,512]{2,1,0:T(8,128)(2,1)S(1)}, bf16[2,272,512]{2,1,0:T(8,128)(2,1)S(1)}, u32[]{:S(2)}, u32[]{:S(2)}) %collective-permute-start.1) | collective-permute-done | bytes 557088 | tf_op jit(solution)/shard_map/ppermute | solution.py:256
  61.3 0.0 copy-start.8
  61.3 8.0 %shard_map.98 = (bf16[512,512]{1,0:T(8,128)(2,1)S(1)}, bf16[512,512]{1,0:T(8,128)(2,1)S(1)}) custom-call(bf16[2,272,512]{2,1,0:T(8,128)(2,1)S(1)} %shard_map.96.own_ref, bf16[2,272,512]{2,1,0:T(8,128)(2,1)S(1)} %collective-permute-done.low_ref, bf16[2,272,512]{2,1,0:T(8,128)(2,1)S(1)} %collective-permute-done.1.high_ref, ...), custom_call_target="tpu_custom_call" | custom-call | flops 2415919104 | bytes 2097152 | tf_op jit(solution)/shard_map/pallas_call | solution.py:204
  69.3 0.0 copy-start.9
  69.4 0.8 copy-done.9
  70.1 0.0 all-gather.3.cloned.1.call-done
  70.1 0.0 copy-done.8
  70.1 0.0 copy-start.2
  70.1 1.6 copy-done.2
  71.7 0.0 copy-start.10
  71.7 1.0 copy-done.10
  72.8 0.0 copy-start.3
  72.8 1.9 %shard_map.100 = (bf16[1024,512]{1,0:T(8,128)(2,1)S(1)}, bf16[2,8,64,512]{3,2,1,0:T(8,128)(2,1)S(1)}) custom-call(s32[1]{0:T(128)S(6)} %sub.3.parity_ref, bf16[512,512]{1,0:T(8,128)(2,1)S(1)} %copy-done.10, bf16[8,2,128,512]{3,2,1,0:T(8,128)(2,1)S(1)} %bitcast.15, bf16[512,512]{1,0:T(8,128)(2,1)S(1)} %copy-done.8), custom_call_target="tpu_custom_call" | custom-call | flops 1073741824 | bytes 4194304 | tf_op jit(solution)/shard_map/pallas_call | solution.py:204
  74.7 2.1 %collective-permute-start.2 = (bf16[2,8,64,512]{3,2,1,0:T(8,128)(2,1)S(1)}, bf16[2,8,64,512]{3,2,1,0:T(8,128)(2,1)S(1)}, u32[]{:S(2)}, u32[]{:S(2)}) collective-permute-start(bf16[2,8,64,512]{3,2,1,0:T(8,128)(2,1)S(1)} %get-tuple-element.27), channel_id=1, source_target_pairs={{0,1},{1,0},{2,3},{3,2},{4,5},{5,4},{6,7},{7,6},{8,9},{9,8},{10,11... | collective-permute-start | bytes 3145736 | tf_op jit(solution)/shard_map/ppermute | solution.py:285
  76.8 0.0 copy-done.3
  76.8 1.9 %shard_map.99 = (bf16[1024,512]{1,0:T(8,128)(2,1)S(1)}, bf16[2,8,64,512]{3,2,1,0:T(8,128)(2,1)S(1)}) custom-call(s32[1]{0:T(128)} %bitcast.parity_ref, bf16[512,512]{1,0:T(8,128)(2,1)S(1)} %copy-done.10, bf16[8,2,128,512]{3,2,1,0:T(8,128)(2,1)S(1)} %bitcast.16, bf16[512,512]{1,0:T(8,128)(2,1)S(1)} %copy-done.8), custom_call_target="tpu_custom_call" | custom-call | flops 1073741824 | bytes 4194304 | tf_op jit(solution)/shard_map/pallas_call | solution.py:204
  78.7 0.5 collective-permute-done.2
  79.2 0.4 add_convert_fusion
  79.6 25.5 %all_to_all.20 = bf16[16,64,512]{2,1,0:T(8,128)(2,1)} all-to-all(bf16[16,64,512]{2,1,0:T(8,128)(2,1)S(1)} %bitcast.18), channel_id=1, replica_groups={{0,2,4,6,8,10,12,14,16,18,20,22,24,26,28,30},{1,3,5,7,9,11,13,15,17,19,..., dimensions={0} | all-to-all | bytes 2097152 | tf_op jit(solution)/shard_map/all_to_all | solution.py:296
  105.1 1.4 reduce_sum.24
  106.5 25.3 %all_to_all.21 = bf16[16,4,512]{2,1,0:T(4,128)(2,1)S(1)} all-to-all(bf16[16,4,512]{2,1,0:T(4,128)(2,1)S(1)} %reshape.34), channel_id=1, replica_groups={{0,32,64,96,128,160,192,224,256,288,320,352,384,416,448,480},{16,48,80,..., dimensions={0} | all-to-all | bytes 131072 | tf_op jit(solution)/shard_map/all_to_all | solution.py:301
  131.8 0.7 broadcast_in_dim.2
  132.5 4.2 %all-to-all-start.3 = ((bf16[32,4,512]{2,1,0:T(4,128)(2,1)}), bf16[32,4,512]{2,1,0:T(4,128)(2,1)S(1)}, u32[]{:S(2)}, u32[]{:S(2)}) async-start(bf16[32,4,512]{2,1,0:T(4,128)(2,1)} %broadcast_in_dim.2), calls=%async_computation.3 | async-start | bytes 262144 | tf_op jit(solution)/shard_map/all_to_all | solution.py:310
  136.7 0.0 all-gather.5.cloned.1.call-done
  136.7 0.0 copy-start
  136.7 1.6 copy-done
  138.3 2.1 %shard_map.101 = bf16[512,512]{1,0:T(8,128)(2,1)} custom-call(s32[1]{0:T(128)} %bitcast.parity_ref, bf16[512,512]{1,0:T(8,128)(2,1)S(1)} %get-tuple-element.21.res_ref, bf16[1024,512]{1,0:T(8,128)(2,1)S(1)} %get-tuple-element.24.one_ref, bf16[1024,512]{1,0:T(8,128)(2,1)S(1)} %get-tuple-element.25.two_ref, bf16[8,2,128,512]{3,2,1,0:T(8,128)(2,1)S(1)} %bitcast.13), custom_call_target="tpu_custom_call" | custom-call | flops 1073741824 | bytes 1048576 | tf_op jit(solution)/shard_map/pallas_call | solution.py:204
  140.4 12.4 %all-to-all-done.3 = bf16[32,4,512]{2,1,0:T(4,128)(2,1)S(1)} async-done(((bf16[32,4,512]{2,1,0:T(4,128)(2,1)}), bf16[32,4,512]{2,1,0:T(4,128)(2,1)S(1)}, u32[]{:S(2)}, u32[]{:S(2)}) %all-to-all-start.3) | async-done | bytes 131104 | tf_op jit(solution)/shard_map/all_to_all | solution.py:310
  152.9 0.8 reshape.35
  (4 shorter events, 0.1 us)
Async XLA Ops:
  7.2 63.0 %all-gather.3.cloned.1.call-start = ((), (), s32[]{:S(2)}) async-start(), calls=%async_computation.4 | async-start | bytes 2228224 | tf_op jit(solution)/shard_map/all_gather | solution.py:226
  7.9 33.1 %copy-start.1 = (s32[1,2,256]{2,1,0:T(2,128)S(1)}, s32[1,2,256]{2,1,0:T(2,128)}, u32[]{:S(2)}) copy-start(s32[1,2,256]{2,1,0:T(2,128)} %param.10) | copy-start | bytes 6148
  11.1 36.0 %copy-start.4 = (bf16[512,1536]{1,0:T(8,128)(2,1)S(1)}, bf16[512,1536]{1,0:T(8,128)(2,1)}, u32[]{:S(2)}) copy-start(bf16[512,1536]{1,0:T(8,128)(2,1)} %w_ref.1) | copy-start | bytes 4718596
  11.1 29.9 %all-to-all-start = ((bf16[16,2,32,640]{3,2,1,0:T(8,128)(2,1)}), bf16[16,2,32,640]{3,2,1,0:T(8,128)(2,1)S(1)}, u32[]{:S(2)}, u32[]{:S(2)}) async-start(bf16[16,2,32,640]{3,2,1,0:T(8,128)(2,1)} %shard_map.95), calls=%async_computation | async-start | bytes 2621440 | tf_op jit(solution)/shard_map/all_to_all | solution.py:246
  20.7 116.1 %all-gather.5.cloned.1.call-start = ((), (), s32[]{:S(2)}) async-start(), calls=%async_computation.5 | async-start | bytes 2228224 | tf_op jit(solution)/shard_map/all_gather | solution.py:227
  41.5 15.2 %collective-permute-start = (bf16[2,272,512]{2,1,0:T(8,128)(2,1)S(1)}, bf16[2,272,512]{2,1,0:T(8,128)(2,1)S(1)}, u32[]{:S(2)}, u32[]{:S(2)}) collective-permute-start(bf16[2,272,512]{2,1,0:T(8,128)(2,1)S(1)} %shard_map.96.own_ref), channel_id=1, source_target_pairs={{0,1},{1,2},{2,3},{3,4},{4,5},{5,6},{6,7},{7,8},{8,9},{9,10},{10,1... | collective-permute-start | bytes 1671176 | tf_op jit(solution)/shard_map/ppermute | solution.py:255
  43.6 17.8 %collective-permute-start.1 = (bf16[2,272,512]{2,1,0:T(8,128)(2,1)S(1)}, bf16[2,272,512]{2,1,0:T(8,128)(2,1)S(1)}, u32[]{:S(2)}, u32[]{:S(2)}) collective-permute-start(bf16[2,272,512]{2,1,0:T(8,128)(2,1)S(1)} %shard_map.96.own_ref), channel_id=1, source_target_pairs={{1,0},{2,1},{3,2},{4,3},{5,4},{6,5},{7,6},{8,7},{9,8},{10,9},{11,1... | collective-permute-start | bytes 1671176 | tf_op jit(solution)/shard_map/ppermute | solution.py:256
  47.1 1.0 copy-start.5
  48.2 1.1 copy-start.6
  52.2 0.8 copy-start.7
  61.3 8.8 %copy-start.8 = (bf16[512,512]{1,0:T(8,128)(2,1)S(1)}, bf16[512,512]{1,0:T(8,128)(2,1)}, u32[]{:S(2)}) copy-start(bf16[512,512]{1,0:T(8,128)(2,1)} %copy-done.7) | copy-start | bytes 1572868
  69.3 0.8 copy-start.9
  70.1 1.6 copy-start.2
  71.7 1.0 copy-start.10
  72.8 4.0 %copy-start.3 = (bf16[2048,512]{1,0:T(8,128)(2,1)S(1)}, bf16[2048,512]{1,0:T(8,128)(2,1)}, u32[]{:S(2)}) copy-start(bf16[2048,512]{1,0:T(8,128)(2,1)} %all-gather.3.cloned.1.call-done) | copy-start | bytes 6291460
  74.7 4.6 %collective-permute-start.2 = (bf16[2,8,64,512]{3,2,1,0:T(8,128)(2,1)S(1)}, bf16[2,8,64,512]{3,2,1,0:T(8,128)(2,1)S(1)}, u32[]{:S(2)}, u32[]{:S(2)}) collective-permute-start(bf16[2,8,64,512]{3,2,1,0:T(8,128)(2,1)S(1)} %get-tuple-element.27), channel_id=1, source_target_pairs={{0,1},{1,0},{2,3},{3,2},{4,5},{5,4},{6,7},{7,6},{8,9},{9,8},{10,11... | collective-permute-start | bytes 3145736 | tf_op jit(solution)/shard_map/ppermute | solution.py:285
  132.5 20.3 %all-to-all-start.3 = ((bf16[32,4,512]{2,1,0:T(4,128)(2,1)}), bf16[32,4,512]{2,1,0:T(4,128)(2,1)S(1)}, u32[]{:S(2)}, u32[]{:S(2)}) async-start(bf16[32,4,512]{2,1,0:T(4,128)(2,1)} %broadcast_in_dim.2), calls=%async_computation.3 | async-start | bytes 262144 | tf_op jit(solution)/shard_map/all_to_all | solution.py:310
  136.7 1.6 copy-start
Sparse Core Ops, SparseCore 0:
  10.1 54.0 all-gather.2
  66.4 49.4 all-gather.4

commit v3 on v2

--- a/solution.py
+++ b/solution.py
@@ -123,7 +123,7 @@
 
 
 def halo_kernel(
-    own_ref, low_ref, high_ref, query_ref, w_ref, w_out_ref, mixed_ref, total_ref, peak_ref, res_ref, normed_ref
+    own_ref, low_ref, high_ref, query_ref, w_ref, w_out_ref, mixed_ref, total_ref, peak_ref, res_ref
 ):
     clouds, length, width = query_ref.shape
     head = width // HEADS
@@ -167,18 +167,17 @@
             part = dot((above / under).astype(BF16), w_out_ref[lanes, :])
             attended = part if h == 0 else attended + part
         residual = (own_ref[c, :length].astype(F32) + attended).astype(BF16)
-        rows = slice(c * length, (c + 1) * length)
-        res_ref[rows] = residual
-        normed_ref[rows] = normalize(residual.astype(F32))
-
-
-def up_kernel(parity_ref, normed_ref, w_up_ref, cot_ref, hidden_ref, grad_ref):
+        res_ref[c * length : (c + 1) * length] = residual
+
+
+def up_kernel(parity_ref, res_ref, w_up_ref, cot_ref, hidden_ref, grad_ref):
     blocks, _, units, _ = w_up_ref.shape
     parity = parity_ref[0]
     half = units // 2
+    normed = normalize(res_ref[...].astype(F32))
     for j in range(0, blocks, 2):
         weights = w_up_ref[j : j + 2, parity].reshape(2 * units, -1)
-        product = dot(weights, normed_ref[...], ((1,), (1,)))
+        product = dot(weights, normed, ((1,), (1,)))
         hidden = jax.nn.gelu(product).astype(BF16)
         hidden_ref[j * units : (j + 2) * units] = hidden
         grad = dot(hidden, cot_ref[...]).astype(BF16)
@@ -267,9 +266,9 @@
     blocks = devices // 2
     up_blocks = up_all.reshape(blocks, 2, units, width)
     halves = [(blocks * units, rows_all), (2, blocks, units // 2, width)]
-    residual, normed_two = call(
+    (residual,) = call(
         halo_kernel,
-        [(flat, BF16), (flat, BF16)],
+        [(flat, BF16)],
         [VMEM] * 9,
         (own, low, high, query, w_kv, w_out, *sums),
         flops=2 * rows_all * width * (5 * width + 8 * length),
@@ -281,9 +280,9 @@
         [SMEM] + [VMEM] * 3,
         flops=4 * rows_all * width * units * blocks,
     )
-    hidden_two, grad_two = up((1 - parity, normed_two, up_blocks, cot_rows))
+    hidden_two, grad_two = up((1 - parity, residual, up_blocks, cot_rows))
     grad_got = lax.ppermute(grad_two, "point", [(i, i ^ 1) for i in range(devices)])
-    hidden_one, grad_one = up((parity, normed_two, up_blocks, cot_rows))
+    hidden_one, grad_one = up((parity, residual, up_blocks, cot_rows))
     grad = (grad_one.astype(F32) + grad_got.astype(F32)).astype(BF16)
     grad = grad.reshape(2 * blocks, units // 2, width)
 

time: 161 us -> 159 us (0.988)
  local copies, waits for them, and re-layouts: 9.44 us -> 7.59 us
    unnamed x22 -> x18, local copies, waits for them, and re-layouts: 7.91 us -> 6.06 us
where the time goes in v3:
time: 159 us
  blocking collectives  50.9 us (32%)
  waiting for transfers between devices  42.1 us (26%)
  starting transfers between devices  21.3 us (13%)
  Pallas kernels  20.8 us (13%)
  between operations  14.2 us (9%)
  local copies, waits for them, and re-layouts  7.59 us (5%)
  other arithmetic  1.82 us (1%)
    all_to_all x1, blocking collectives, on_device(): lax.all_to_all(grad.reshape(stages, piece, width), 'dp', 0, 0, axis_index...  25.7 us
    all_to_all x1, blocking collectives, on_device(): lax.all_to_all(grad, ('dp', 'point'), 0, 0, axis_index_groups=planes, til...  25.2 us
    pallas_call x7, Pallas kernels, call(): pl.pallas_call(kernel, out_shape=[jax.ShapeDtypeStruct(shape, kind) for s...  20.8 us
    all_to_all x1, waiting for transfers between devices, on_device(): arrived = lax.all_to_all(outgoing, 'point', 0, 0, tiled=True)  19.6 us
    all_to_all x1, waiting for transfers between devices, on_device(): lax.all_to_all(jnp.broadcast_to(grad[None], (groups, piece, width)), 'dp'...  12.5 us
    all_to_all x1, starting transfers between devices, on_device(): arrived = lax.all_to_all(outgoing, 'point', 0, 0, tiled=True)  9.55 us
    unnamed x18, local copies, waits for them, and re-layouts  6.06 us
    ppermute x1, waiting for transfers between devices, on_device(): high = lax.ppermute(own, 'point', backward)  4.56 us
  transfers between devices with their start and end apart: 7, of which 5 were waited for; matrix products, arithmetic and copies ran while one was open for 2% of the time, Pallas kernels for 13%

profile of v3, /device:TPU:2, one launch (start us, length us, event | category | flops | bytes accessed | tf_op | source)
XLA Modules:
  0.0 158.8 jit_solution(8629631882669460639)
XLA Ops:
  7.2 0.0 all-gather.3.cloned.1.call-start
  7.2 0.7 all-gather.3.cloned.1.call-update
  7.9 0.0 copy-start.1
  7.9 3.2 %shard_map.95 = bf16[16,2,32,640]{3,2,1,0:T(8,128)(2,1)} custom-call(s32[2,256]{1,0:T(2,128)} %bitcast.22, bf16[2,256,512]{2,1,0:T(8,128)(2,1)} %bitcast.20), custom_call_target="tpu_custom_call" | custom-call | flops 268435456 | bytes 2621440 | tf_op jit(solution)/shard_map/pallas_call | solution.py:203
  11.1 0.0 copy-start.4
  11.1 9.5 %all-to-all-start = ((bf16[16,2,32,640]{3,2,1,0:T(8,128)(2,1)}), bf16[16,2,32,640]{3,2,1,0:T(8,128)(2,1)S(1)}, u32[]{:S(2)}, u32[]{:S(2)}) async-start(bf16[16,2,32,640]{3,2,1,0:T(8,128)(2,1)} %shard_map.95), calls=%async_computation | async-start | bytes 2621440 | tf_op jit(solution)/shard_map/all_to_all | solution.py:245
  20.7 0.0 all-gather.5.cloned.1.call-start
  20.7 0.7 all-gather.5.cloned.1.call-update
  21.4 19.6 %all-to-all-done.arrived_ref = bf16[16,2,32,640]{3,2,1,0:T(8,128)(2,1)S(1)} async-done(((bf16[16,2,32,640]{3,2,1,0:T(8,128)(2,1)}), bf16[16,2,32,640]{3,2,1,0:T(8,128)(2,1)S(1)}, u32[]{:S(2)}, u32[]{:S(2)}) %all-to-all-start) | async-done | bytes 1310752 | tf_op jit(solution)/shard_map/all_to_all | solution.py:245
  41.0 0.0 copy-done.1
  41.1 0.5 shard_map.96.own_ref
  41.5 2.0 %collective-permute-start = (bf16[2,272,512]{2,1,0:T(8,128)(2,1)S(1)}, bf16[2,272,512]{2,1,0:T(8,128)(2,1)S(1)}, u32[]{:S(2)}, u32[]{:S(2)}) collective-permute-start(bf16[2,272,512]{2,1,0:T(8,128)(2,1)S(1)} %shard_map.96.own_ref), channel_id=1, source_target_pairs={{0,1},{1,2},{2,3},{3,4},{4,5},{5,6},{6,7},{7,8},{8,9},{9,10},{10,1... | collective-permute-start | bytes 1671176 | tf_op jit(solution)/shard_map/ppermute | solution.py:254
  43.6 3.5 %collective-permute-start.1 = (bf16[2,272,512]{2,1,0:T(8,128)(2,1)S(1)}, bf16[2,272,512]{2,1,0:T(8,128)(2,1)S(1)}, u32[]{:S(2)}, u32[]{:S(2)}) collective-permute-start(bf16[2,272,512]{2,1,0:T(8,128)(2,1)S(1)} %shard_map.96.own_ref), channel_id=1, source_target_pairs={{1,0},{2,1},{3,2},{4,3},{5,4},{6,5},{7,6},{8,7},{9,8},{10,9},{11,1... | collective-permute-start | bytes 1671176 | tf_op jit(solution)/shard_map/ppermute | solution.py:255
  47.1 0.0 copy-done.4
  47.1 0.0 copy-start.5
  47.1 1.0 copy-done.5
  48.2 0.0 copy-start.6
  48.2 1.0 copy-done.6
  49.2 3.0 %shard_map.97 = (bf16[2,256,512]{2,1,0:T(8,128)(2,1)S(1)}, bf16[512,1024]{1,0:T(8,128)(2,1)S(1)}, bf16[512,512]{1,0:T(8,128)(2,1)S(1)}, bf16[512,512]{1,0:T(8,12...) custom-call(bf16[2,272,512]{2,1,0:T(8,128)(2,1)S(1)} %shard_map.96.own_ref, ...), custom_call_target="tpu_custom_call" | custom-call | flops 1342177280 | bytes 8388608 | tf_op jit(solution)/shard_map/pallas_call | solution.py:203
  52.2 0.0 copy-start.7
  52.2 0.8 copy-done.7
  53.0 3.7 %collective-permute-done.low_ref = bf16[2,272,512]{2,1,0:T(8,128)(2,1)S(1)} collective-permute-done((bf16[2,272,512]{2,1,0:T(8,128)(2,1)S(1)}, bf16[2,272,512]{2,1,0:T(8,128)(2,1)S(1)}, u32[]{:S(2)}, u32[]{:S(2)}) %collective-permute-start) | collective-permute-done | bytes 557088 | tf_op jit(solution)/shard_map/ppermute | solution.py:254
  56.8 4.6 %collective-permute-done.1.high_ref = bf16[2,272,512]{2,1,0:T(8,128)(2,1)S(1)} collective-permute-done((bf16[2,272,512]{2,1,0:T(8,128)(2,1)S(1)}, bf16[2,272,512]{2,1,0:T(8,128)(2,1)S(1)}, u32[]{:S(2)}, u32[]{:S(2)}) %collective-permute-start.1) | collective-permute-done | bytes 557088 | tf_op jit(solution)/shard_map/ppermute | solution.py:255
  61.3 0.0 copy-start.8
  61.3 7.8 %shard_map.98.res_ref = bf16[512,512]{1,0:T(8,128)(2,1)S(1)} custom-call(bf16[2,272,512]{2,1,0:T(8,128)(2,1)S(1)} %shard_map.96.own_ref, bf16[2,272,512]{2,1,0:T(8,128)(2,1)S(1)} %collective-permute-done.low_ref, bf16[2,272,512]{2,1,0:T(8,128)(2,1)S(1)} %collective-permute-done.1.high_ref, bf16[2,256,512]{2,1,0:T(8,128)(2,1)S(1)} %get-tuple-element.13.query_ref, ...), custom_call_target="tpu_custom_call" | custom-call | flops 2415919104 | bytes 1048576 | tf_op jit(solution)/shard_map/pallas_call | solution.py:203
  69.2 0.0 all-gather.3.cloned.1.call-done
  69.2 0.0 copy-done.8
  69.2 0.0 copy-start.2
  69.2 1.6 copy-done.2
  70.8 0.0 copy-start.3
  70.8 2.1 %shard_map.100 = (bf16[1024,512]{1,0:T(8,128)(2,1)S(1)}, bf16[2,8,64,512]{3,2,1,0:T(8,128)(2,1)S(1)}) custom-call(s32[1]{0:T(128)S(6)} %sub.3.parity_ref, bf16[512,512]{1,0:T(8,128)(2,1)S(1)} %shard_map.98.res_ref, bf16[8,2,128,512]{3,2,1,0:T(8,128)(2,1)S(1)} %bitcast.15, bf16[512,512]{1,0:T(8,128)(2,1)S(1)} %copy-done.8), custom_call_target="tpu_custom_call" | custom-call | flops 1073741824 | bytes 4194304 | tf_op jit(solution)/shard_map/pallas_call | solution.py:203
  72.9 2.1 %collective-permute-start.2 = (bf16[2,8,64,512]{3,2,1,0:T(8,128)(2,1)S(1)}, bf16[2,8,64,512]{3,2,1,0:T(8,128)(2,1)S(1)}, u32[]{:S(2)}, u32[]{:S(2)}) collective-permute-start(bf16[2,8,64,512]{3,2,1,0:T(8,128)(2,1)S(1)} %get-tuple-element.23), channel_id=1, source_target_pairs={{0,1},{1,0},{2,3},{3,2},{4,5},{5,4},{6,7},{7,6},{8,9},{9,8},{10,11... | collective-permute-start | bytes 3145736 | tf_op jit(solution)/shard_map/ppermute | solution.py:284
  75.0 0.0 copy-done.3
  75.0 2.1 %shard_map.99 = (bf16[1024,512]{1,0:T(8,128)(2,1)S(1)}, bf16[2,8,64,512]{3,2,1,0:T(8,128)(2,1)S(1)}) custom-call(s32[1]{0:T(128)} %bitcast.parity_ref, bf16[512,512]{1,0:T(8,128)(2,1)S(1)} %shard_map.98.res_ref, bf16[8,2,128,512]{3,2,1,0:T(8,128)(2,1)S(1)} %bitcast.16, bf16[512,512]{1,0:T(8,128)(2,1)S(1)} %copy-done.8), custom_call_target="tpu_custom_call" | custom-call | flops 1073741824 | bytes 4194304 | tf_op jit(solution)/shard_map/pallas_call | solution.py:203
  77.1 0.3 collective-permute-done.2
  77.4 0.4 add_convert_fusion
  77.8 25.2 %all_to_all.20 = bf16[16,64,512]{2,1,0:T(8,128)(2,1)} all-to-all(bf16[16,64,512]{2,1,0:T(8,128)(2,1)S(1)} %bitcast.18), channel_id=1, replica_groups={{0,2,4,6,8,10,12,14,16,18,20,22,24,26,28,30},{1,3,5,7,9,11,13,15,17,19,..., dimensions={0} | all-to-all | bytes 2097152 | tf_op jit(solution)/shard_map/all_to_all | solution.py:295
  103.0 1.4 reduce_sum.24
  104.4 25.7 %all_to_all.21 = bf16[16,4,512]{2,1,0:T(4,128)(2,1)S(1)} all-to-all(bf16[16,4,512]{2,1,0:T(4,128)(2,1)S(1)} %reshape.34), channel_id=1, replica_groups={{0,32,64,96,128,160,192,224,256,288,320,352,384,416,448,480},{16,48,80,..., dimensions={0} | all-to-all | bytes 131072 | tf_op jit(solution)/shard_map/all_to_all | solution.py:300
  130.2 0.7 broadcast_in_dim.2
  130.9 4.0 %all-to-all-start.3 = ((bf16[32,4,512]{2,1,0:T(4,128)(2,1)}), bf16[32,4,512]{2,1,0:T(4,128)(2,1)S(1)}, u32[]{:S(2)}, u32[]{:S(2)}) async-start(bf16[32,4,512]{2,1,0:T(4,128)(2,1)} %broadcast_in_dim.2), calls=%async_computation.3 | async-start | bytes 262144 | tf_op jit(solution)/shard_map/all_to_all | solution.py:309
  134.9 0.0 all-gather.5.cloned.1.call-done
  135.0 0.0 copy-start
  135.0 1.6 copy-done
  136.6 2.1 %shard_map.101 = bf16[512,512]{1,0:T(8,128)(2,1)} custom-call(s32[1]{0:T(128)} %bitcast.parity_ref, bf16[512,512]{1,0:T(8,128)(2,1)S(1)} %shard_map.98.res_ref, bf16[1024,512]{1,0:T(8,128)(2,1)S(1)} %get-tuple-element.20.one_ref, bf16[1024,512]{1,0:T(8,128)(2,1)S(1)} %get-tuple-element.21.two_ref, bf16[8,2,128,512]{3,2,1,0:T(8,128)(2,1)S(1)} %bitcast.13), custom_call_target="tpu_custom_call" | custom-call | flops 1073741824 | bytes 1048576 | tf_op jit(solution)/shard_map/pallas_call | solution.py:203
  138.6 12.5 %all-to-all-done.3 = bf16[32,4,512]{2,1,0:T(4,128)(2,1)S(1)} async-done(((bf16[32,4,512]{2,1,0:T(4,128)(2,1)}), bf16[32,4,512]{2,1,0:T(4,128)(2,1)S(1)}, u32[]{:S(2)}, u32[]{:S(2)}) %all-to-all-start.3) | async-done | bytes 131104 | tf_op jit(solution)/shard_map/all_to_all | solution.py:309
  151.2 0.8 reshape.35
  (4 shorter events, 0.1 us)
Async XLA Ops:
  7.2 62.0 %all-gather.3.cloned.1.call-start = ((), (), s32[]{:S(2)}) async-start(), calls=%async_computation.4 | async-start | bytes 2228224 | tf_op jit(solution)/shard_map/all_gather | solution.py:225
  7.9 33.2 %copy-start.1 = (s32[1,2,256]{2,1,0:T(2,128)S(1)}, s32[1,2,256]{2,1,0:T(2,128)}, u32[]{:S(2)}) copy-start(s32[1,2,256]{2,1,0:T(2,128)} %param.10) | copy-start | bytes 6148
  11.1 36.0 %copy-start.4 = (bf16[512,1536]{1,0:T(8,128)(2,1)S(1)}, bf16[512,1536]{1,0:T(8,128)(2,1)}, u32[]{:S(2)}) copy-start(bf16[512,1536]{1,0:T(8,128)(2,1)} %w_ref.1) | copy-start | bytes 4718596
  11.1 29.9 %all-to-all-start = ((bf16[16,2,32,640]{3,2,1,0:T(8,128)(2,1)}), bf16[16,2,32,640]{3,2,1,0:T(8,128)(2,1)S(1)}, u32[]{:S(2)}, u32[]{:S(2)}) async-start(bf16[16,2,32,640]{3,2,1,0:T(8,128)(2,1)} %shard_map.95), calls=%async_computation | async-start | bytes 2621440 | tf_op jit(solution)/shard_map/all_to_all | solution.py:245
  20.7 114.3 %all-gather.5.cloned.1.call-start = ((), (), s32[]{:S(2)}) async-start(), calls=%async_computation.5 | async-start | bytes 2228224 | tf_op jit(solution)/shard_map/all_gather | solution.py:226
  41.5 15.2 %collective-permute-start = (bf16[2,272,512]{2,1,0:T(8,128)(2,1)S(1)}, bf16[2,272,512]{2,1,0:T(8,128)(2,1)S(1)}, u32[]{:S(2)}, u32[]{:S(2)}) collective-permute-start(bf16[2,272,512]{2,1,0:T(8,128)(2,1)S(1)} %shard_map.96.own_ref), channel_id=1, source_target_pairs={{0,1},{1,2},{2,3},{3,4},{4,5},{5,6},{6,7},{7,8},{8,9},{9,10},{10,1... | collective-permute-start | bytes 1671176 | tf_op jit(solution)/shard_map/ppermute | solution.py:254
  43.6 17.8 %collective-permute-start.1 = (bf16[2,272,512]{2,1,0:T(8,128)(2,1)S(1)}, bf16[2,272,512]{2,1,0:T(8,128)(2,1)S(1)}, u32[]{:S(2)}, u32[]{:S(2)}) collective-permute-start(bf16[2,272,512]{2,1,0:T(8,128)(2,1)S(1)} %shard_map.96.own_ref), channel_id=1, source_target_pairs={{1,0},{2,1},{3,2},{4,3},{5,4},{6,5},{7,6},{8,7},{9,8},{10,9},{11,1... | collective-permute-start | bytes 1671176 | tf_op jit(solution)/shard_map/ppermute | solution.py:255
  47.1 1.0 copy-start.5
  48.2 1.1 copy-start.6
  52.2 0.8 copy-start.7
  61.3 7.9 %copy-start.8 = (bf16[512,512]{1,0:T(8,128)(2,1)S(1)}, bf16[512,512]{1,0:T(8,128)(2,1)}, u32[]{:S(2)}) copy-start(bf16[512,512]{1,0:T(8,128)(2,1)} %copy-done.7) | copy-start | bytes 1572868
  69.2 1.6 %copy-start.2 = (bf16[2048,512]{1,0:T(8,128)(2,1)S(1)}, bf16[2048,512]{1,0:T(8,128)(2,1)}, u32[]{:S(2)}) copy-start(bf16[2048,512]{1,0:T(8,128)(2,1)} %all-gather.3.cloned.1.call-done) | copy-start | bytes 6291460
  70.8 4.2 %copy-start.3 = (bf16[2048,512]{1,0:T(8,128)(2,1)S(1)}, bf16[2048,512]{1,0:T(8,128)(2,1)}, u32[]{:S(2)}) copy-start(bf16[2048,512]{1,0:T(8,128)(2,1)} %all-gather.3.cloned.1.call-done) | copy-start | bytes 6291460
  72.9 4.6 %collective-permute-start.2 = (bf16[2,8,64,512]{3,2,1,0:T(8,128)(2,1)S(1)}, bf16[2,8,64,512]{3,2,1,0:T(8,128)(2,1)S(1)}, u32[]{:S(2)}, u32[]{:S(2)}) collective-permute-start(bf16[2,8,64,512]{3,2,1,0:T(8,128)(2,1)S(1)} %get-tuple-element.23), channel_id=1, source_target_pairs={{0,1},{1,0},{2,3},{3,2},{4,5},{5,4},{6,7},{7,6},{8,9},{9,8},{10,11... | collective-permute-start | bytes 3145736 | tf_op jit(solution)/shard_map/ppermute | solution.py:284
  130.9 20.2 %all-to-all-start.3 = ((bf16[32,4,512]{2,1,0:T(4,128)(2,1)}), bf16[32,4,512]{2,1,0:T(4,128)(2,1)S(1)}, u32[]{:S(2)}, u32[]{:S(2)}) async-start(bf16[32,4,512]{2,1,0:T(4,128)(2,1)} %broadcast_in_dim.2), calls=%async_computation.3 | async-start | bytes 262144 | tf_op jit(solution)/shard_map/all_to_all | solution.py:309
  135.0 1.6 %copy-start = (bf16[2048,512]{1,0:T(8,128)(2,1)S(1)}, bf16[2048,512]{1,0:T(8,128)(2,1)}, u32[]{:S(2)}) copy-start(bf16[2048,512]{1,0:T(8,128)(2,1)} %all-gather.5.cloned.1.call-done) | copy-start | bytes 6291460
Sparse Core Ops, SparseCore 0:
  10.1 54.0 all-gather.2
  66.4 49.8 all-gather.4

commit v4 on v3

--- a/solution.py
+++ b/solution.py
@@ -122,8 +122,8 @@
     cot_copy_ref[...] = cot_ref[...]
 
 
-def halo_kernel(
-    own_ref, low_ref, high_ref, query_ref, w_ref, w_out_ref, mixed_ref, total_ref, peak_ref, res_ref
+def low_kernel(
+    own_ref, low_ref, query_ref, w_ref, mixed_ref, total_ref, peak_ref, mixed_out, total_out, peak_out
 ):
     clouds, length, width = query_ref.shape
     head = width // HEADS
@@ -132,7 +132,7 @@
     scale = head ** (-0.5) * LOG2E
     for c in range(clouds):
         sides = []
-        for ref in (low_ref, high_ref):
+        for ref in (low_ref,):
             normed = normalize(ref[c, :length].astype(F32))
             sides.append((dot(normed, w_ref[...]).astype(BF16), tags_of(ref[c], length)))
         asks = column(tags_of(own_ref[c], length))
@@ -150,7 +150,54 @@
                     jnp.where(ok, dot(asked, kv[:, lanes], ((1,), (1,))), -1e30)
                     for (kv, _), ok in zip(sides, allowed)
                 ]
-                best = jnp.max(jnp.maximum(scores[0], scores[1]), axis=1, keepdims=True)
+                best = jnp.max(scores[0], axis=1, keepdims=True)
+                best = jnp.maximum(best, old_peak[:, k * head : k * head + 1])
+                part = None
+                for (kv, _), s in zip(sides, scores):
+                    weights = jnp.exp2((s - best) * scale).astype(BF16)
+                    add = dot(weights, jnp.concatenate([kv[:, values], ones], axis=1))
+                    part = add if part is None else part + add
+                sums.append(part)
+                peaks.append(best)
+            fade = jnp.exp2((old_peak - jnp.where(first, peaks[0], peaks[1])) * scale)
+            above = jnp.where(first, sums[0][:, :LANES], sums[1][:, :LANES])
+            under = jnp.where(first, sums[0][:, LANES:], sums[1][:, LANES:])
+            above += mixed_ref[c, :, lanes] * fade
+            under += total_ref[c, :, lanes] * fade
+            mixed_out[c, :, lanes] = above
+            total_out[c, :, lanes] = under
+            peak_out[c, :, lanes] = jnp.where(first, peaks[0], peaks[1])
+
+
+def halo_kernel(
+    own_ref, high_ref, query_ref, w_ref, w_out_ref, mixed_ref, total_ref, peak_ref, res_ref
+):
+    clouds, length, width = query_ref.shape
+    head = width // HEADS
+    first = lax.broadcasted_iota(jnp.int32, (length, LANES), 1) < head
+    ones = jnp.ones((length, LANES), BF16)
+    scale = head ** (-0.5) * LOG2E
+    for c in range(clouds):
+        sides = []
+        for ref in (high_ref,):
+            normed = normalize(ref[c, :length].astype(F32))
+            sides.append((dot(normed, w_ref[...]).astype(BF16), tags_of(ref[c], length)))
+        asks = column(tags_of(own_ref[c], length))
+        asks = jnp.concatenate([asks] * (length // LANES), axis=1)
+        allowed = [asks == tags for _, tags in sides]
+        for h in range(width // LANES):
+            lanes = slice(h * LANES, (h + 1) * LANES)
+            values = slice(width + h * LANES, width + (h + 1) * LANES)
+            queries = query_ref[c, :, lanes]
+            old_peak = peak_ref[c, :, lanes]
+            peaks, sums = [], []
+            for k, inside in enumerate((first, ~first)):
+                asked = jnp.where(inside, queries, jnp.zeros_like(queries))
+                scores = [
+                    jnp.where(ok, dot(asked, kv[:, lanes], ((1,), (1,))), -1e30)
+                    for (kv, _), ok in zip(sides, allowed)
+                ]
+                best = jnp.max(scores[0], axis=1, keepdims=True)
                 best = jnp.maximum(best, old_peak[:, k * head : k * head + 1])
                 part = None
                 for (kv, _), s in zip(sides, scores):
@@ -266,11 +313,18 @@
     blocks = devices // 2
     up_blocks = up_all.reshape(blocks, 2, units, width)
     halves = [(blocks * units, rows_all), (2, blocks, units // 2, width)]
+    sums = call(
+        low_kernel,
+        [(each, F32)] * 3,
+        [VMEM] * 7,
+        (own, low, query, w_kv, *sums),
+        flops=2 * rows_all * width * (2 * width + 4 * length),
+    )
     (residual,) = call(
         halo_kernel,
         [(flat, BF16)],
-        [VMEM] * 9,
-        (own, low, high, query, w_kv, w_out, *sums),
+        [VMEM] * 8,
+        (own, high, query, w_kv, w_out, *sums),
         flops=2 * rows_all * width * (5 * width + 8 * length),
     )
     up = partial(

time: 159 us -> 161 us (1.013)
  blocking collectives: 50.9 us -> 80.3 us
  waiting for transfers between devices: 42.1 us -> 18.4 us
  starting transfers between devices: 21.3 us -> 14 us
  Pallas kernels: 20.8 us -> 24 us
    all_to_all x0 -> x1, blocking collectives: none -> 29.8 us  [on_device(): arrived = lax.all_to_all(outgoing, 'point', 0, 0, tiled=True)]
    all_to_all x1 -> x0, waiting for transfers between devices: 19.6 us -> none  [on_device(): arrived = lax.all_to_all(outgoing, 'point', 0, 0, tiled=True)]
    all_to_all x1 -> x0, starting transfers between devices: 9.55 us -> none  [on_device(): arrived = lax.all_to_all(outgoing, 'point', 0, 0, tiled=True)]
    ppermute x1, waiting for transfers between devices: 4.56 us -> 0.01 us  [on_device(): high = lax.ppermute(own, 'point', backward)]
    pallas_call x7 -> x8, Pallas kernels: 20.8 us -> 24 us  [call(): pl.pallas_call(kernel, out_shape=[jax.ShapeDtypeStruct(shape, kind) for s...]
    ppermute x1, starting transfers between devices: 2.1 us -> 3.89 us  [on_device(): lax.ppermute(grad_two, 'point', [(i, i ^ 1) for i in range(devices)])]
    unnamed x18 -> x20, local copies, waits for them, and re-layouts: 6.06 us -> 6.32 us
  transfers between devices with their start and end apart: 7 -> 6, of which waited for: 5 -> 2; matrix products, arithmetic and copies ran while one was open for 2% -> 2% of each run, Pallas kernels for 13% -> 15%
where the time goes in v4:
time: 161 us
  blocking collectives  80.3 us (50%)
  Pallas kernels  24 us (15%)
  waiting for transfers between devices  18.4 us (11%)
  between operations  14.3 us (9%)
  starting transfers between devices  14 us (9%)
  local copies, waits for them, and re-layouts  7.85 us (5%)
  other arithmetic  1.79 us (1%)
    all_to_all x1, blocking collectives, on_device(): arrived = lax.all_to_all(outgoing, 'point', 0, 0, tiled=True)  29.8 us
    all_to_all x1, blocking collectives, on_device(): lax.all_to_all(grad, ('dp', 'point'), 0, 0, axis_index_groups=planes, til...  25.4 us
    all_to_all x1, blocking collectives, on_device(): lax.all_to_all(grad.reshape(stages, piece, width), 'dp', 0, 0, axis_index...  25.1 us
    pallas_call x8, Pallas kernels, call(): pl.pallas_call(kernel, out_shape=[jax.ShapeDtypeStruct(shape, kind) for s...  24 us
    all_to_all x1, waiting for transfers between devices, on_device(): lax.all_to_all(jnp.broadcast_to(grad[None], (groups, piece, width)), 'dp'...  13.5 us
    unnamed x20, local copies, waits for them, and re-layouts  6.32 us
    all_to_all x1, starting transfers between devices, on_device(): lax.all_to_all(jnp.broadcast_to(grad[None], (groups, piece, width)), 'dp'...  4.48 us
    ppermute x1, waiting for transfers between devices, on_device(): low = lax.ppermute(own, 'point', forward)  4.21 us
  transfers between devices with their start and end apart: 6, of which 2 were waited for; matrix products, arithmetic and copies ran while one was open for 2% of the time, Pallas kernels for 15%

profile of v4, /device:TPU:2, one launch (start us, length us, event | category | flops | bytes accessed | tf_op | source)
XLA Modules:
  0.0 160.7 jit_solution(11536670311141079873)
XLA Ops:
  7.2 0.0 all-gather.3.cloned.1.call-start
  7.2 0.7 all-gather.3.cloned.1.call-update
  7.9 0.0 all-gather.5.cloned.1.call-start
  7.9 0.0 copy-start.1
  8.0 3.1 %shard_map.95 = bf16[16,2,32,640]{3,2,1,0:T(8,128)(2,1)} custom-call(s32[2,256]{1,0:T(2,128)} %bitcast.22, bf16[2,256,512]{2,1,0:T(8,128)(2,1)} %bitcast.20), custom_call_target="tpu_custom_call" | custom-call | flops 268435456 | bytes 2621440 | tf_op jit(solution)/shard_map/pallas_call | solution.py:250
  11.1 0.0 copy-start.4
  11.1 29.8 %all_to_all.20.arrived_ref = bf16[16,2,32,640]{3,2,1,0:T(8,128)(2,1)S(1)} all-to-all(bf16[16,2,32,640]{3,2,1,0:T(8,128)(2,1)} %shard_map.95), channel_id=1, replica_groups=mesh['dp'=32,'point'=16] {'point'}, dimensions={0} | all-to-all | bytes 2621440 | tf_op jit(solution)/shard_map/all_to_all | solution.py:292
  40.9 0.0 copy-done.1
  41.0 0.5 shard_map.96.own_ref
  41.4 2.0 %collective-permute-start.1 = (bf16[2,272,512]{2,1,0:T(8,128)(2,1)S(1)}, bf16[2,272,512]{2,1,0:T(8,128)(2,1)S(1)}, u32[]{:S(2)}, u32[]{:S(2)}) collective-permute-start(bf16[2,272,512]{2,1,0:T(8,128)(2,1)S(1)} %shard_map.96.own_ref), channel_id=1, source_target_pairs={{0,1},{1,2},{2,3},{3,4},{4,5},{5,6},{6,7},{7,8},{8,9},{9,10},{10,1... | collective-permute-start | bytes 1671176 | tf_op jit(solution)/shard_map/ppermute | solution.py:301
  43.5 0.0 all-gather.5.cloned.1.call-update
  43.5 3.5 %collective-permute-start = (bf16[2,272,512]{2,1,0:T(8,128)(2,1)S(1)}, bf16[2,272,512]{2,1,0:T(8,128)(2,1)S(1)}, u32[]{:S(2)}, u32[]{:S(2)}) collective-permute-start(bf16[2,272,512]{2,1,0:T(8,128)(2,1)S(1)} %shard_map.96.own_ref), channel_id=1, source_target_pairs={{1,0},{2,1},{3,2},{4,3},{5,4},{6,5},{7,6},{8,7},{9,8},{10,9},{11,1... | collective-permute-start | bytes 1671176 | tf_op jit(solution)/shard_map/ppermute | solution.py:302
  47.0 0.0 copy-done.4
  47.1 0.0 copy-start.5
  47.1 1.0 copy-done.5
  48.1 0.0 copy-start.6
  48.1 1.0 copy-done.6
  49.2 2.9 %shard_map.97 = (bf16[2,256,512]{2,1,0:T(8,128)(2,1)S(1)}, bf16[512,1024]{1,0:T(8,128)(2,1)S(1)}, bf16[512,512]{1,0:T(8,128)(2,1)S(1)}, bf16[512,512]{1,0:T(8,12...) custom-call(bf16[2,272,512]{2,1,0:T(8,128)(2,1)S(1)} %shard_map.96.own_ref, ...), custom_call_target="tpu_custom_call" | custom-call | flops 1342177280 | bytes 8388608 | tf_op jit(solution)/shard_map/pallas_call | solution.py:250
  52.1 0.0 copy-start.7
  52.1 4.2 %collective-permute-done.1.low_ref = bf16[2,272,512]{2,1,0:T(8,128)(2,1)S(1)} collective-permute-done((bf16[2,272,512]{2,1,0:T(8,128)(2,1)S(1)}, bf16[2,272,512]{2,1,0:T(8,128)(2,1)S(1)}, u32[]{:S(2)}, u32[]{:S(2)}) %collective-permute-start.1) | collective-permute-done | bytes 557088 | tf_op jit(solution)/shard_map/ppermute | solution.py:301
  56.3 5.2 %shard_map.98 = (f32[2,256,512]{2,1,0:T(8,128)S(1)}, f32[2,256,512]{2,1,0:T(8,128)S(1)}, f32[2,256,512]{2,1,0:T(8,128)S(1)}) custom-call(bf16[2,272,512]{2,1,0:T(8,128)(2,1)S(1)} %shard_map.96.own_ref, bf16[2,272,512]{2,1,0:T(8,128)(2,1)S(1)} %collective-permute-done.1.low_ref, bf16[2,256,512]{2,1,0:T(8,128)(2,1)S(1)} %get-tuple-element.16.query_ref, ...), custom_call_target="tpu_custom_call" | custom-call | flops 1073741824 | bytes 3145728 | tf_op jit(solution)/shard_map/pallas_call | solution.py:250
  61.6 0.0 copy-done.7
  61.6 0.0 collective-permute-done.high_ref
  61.6 0.0 copy-start.8
  61.6 5.8 %shard_map.99.res_ref = bf16[512,512]{1,0:T(8,128)(2,1)S(1)} custom-call(bf16[2,272,512]{2,1,0:T(8,128)(2,1)S(1)} %shard_map.96.own_ref, bf16[2,272,512]{2,1,0:T(8,128)(2,1)S(1)} %collective-permute-done.high_ref, bf16[2,256,512]{2,1,0:T(8,128)(2,1)S(1)} %get-tuple-element.16.query_ref, bf16[512,1024]{1,0:T(8,128)(2,1)S(1)} %get-tuple-element.17.w_ref, ...), custom_call_target="tpu_custom_call" | custom-call | flops 2415919104 | bytes 1048576 | tf_op jit(solution)/shard_map/pallas_call | solution.py:250
  67.4 0.0 all-gather.3.cloned.1.call-done
  67.4 0.0 copy-done.8
  67.4 0.0 copy-start.2
  67.4 1.6 copy-done.2
  69.0 0.0 copy-start.3
  69.0 2.3 %shard_map.101 = (bf16[1024,512]{1,0:T(8,128)(2,1)S(1)}, bf16[2,8,64,512]{3,2,1,0:T(8,128)(2,1)S(1)}) custom-call(s32[1]{0:T(128)S(6)} %sub.3.parity_ref, bf16[512,512]{1,0:T(8,128)(2,1)S(1)} %shard_map.99.res_ref, bf16[8,2,128,512]{3,2,1,0:T(8,128)(2,1)S(1)} %bitcast.15, bf16[512,512]{1,0:T(8,128)(2,1)S(1)} %copy-done.8), custom_call_target="tpu_custom_call" | custom-call | flops 1073741824 | bytes 4194304 | tf_op jit(solution)/shard_map/pallas_call | solution.py:250
  71.3 3.9 %collective-permute-start.2 = (bf16[2,8,64,512]{3,2,1,0:T(8,128)(2,1)S(1)}, bf16[2,8,64,512]{3,2,1,0:T(8,128)(2,1)S(1)}, u32[]{:S(2)}, u32[]{:S(2)}) collective-permute-start(bf16[2,8,64,512]{3,2,1,0:T(8,128)(2,1)S(1)} %get-tuple-element.29), channel_id=1, source_target_pairs={{0,1},{1,0},{2,3},{3,2},{4,5},{5,4},{6,7},{7,6},{8,9},{9,8},{10,11... | collective-permute-start | bytes 3145736 | tf_op jit(solution)/shard_map/ppermute | solution.py:338
  75.2 0.0 copy-done.3
  75.2 0.0 copy-start.9
  75.2 1.0 copy-done.9
  76.2 2.1 %shard_map.100 = (bf16[1024,512]{1,0:T(8,128)(2,1)S(1)}, bf16[2,8,64,512]{3,2,1,0:T(8,128)(2,1)S(1)}) custom-call(s32[1]{0:T(128)} %bitcast.parity_ref, bf16[512,512]{1,0:T(8,128)(2,1)S(1)} %shard_map.99.res_ref, bf16[8,2,128,512]{3,2,1,0:T(8,128)(2,1)S(1)} %bitcast.16, bf16[512,512]{1,0:T(8,128)(2,1)S(1)} %copy-done.9), custom_call_target="tpu_custom_call" | custom-call | flops 1073741824 | bytes 4194304 | tf_op jit(solution)/shard_map/pallas_call | solution.py:250
  78.3 0.0 collective-permute-done.2
  78.4 0.3 add_convert_fusion
  78.7 25.4 %all_to_all.21 = bf16[16,64,512]{2,1,0:T(8,128)(2,1)} all-to-all(bf16[16,64,512]{2,1,0:T(8,128)(2,1)S(1)} %bitcast.18), channel_id=1, replica_groups={{0,2,4,6,8,10,12,14,16,18,20,22,24,26,28,30},{1,3,5,7,9,11,13,15,17,19,..., dimensions={0} | all-to-all | bytes 2097152 | tf_op jit(solution)/shard_map/all_to_all | solution.py:349
  104.1 1.4 reduce_sum.24
  105.5 25.1 %all_to_all.22 = bf16[16,4,512]{2,1,0:T(4,128)(2,1)S(1)} all-to-all(bf16[16,4,512]{2,1,0:T(4,128)(2,1)S(1)} %reshape.34), channel_id=1, replica_groups={{0,32,64,96,128,160,192,224,256,288,320,352,384,416,448,480},{16,48,80,..., dimensions={0} | all-to-all | bytes 131072 | tf_op jit(solution)/shard_map/all_to_all | solution.py:354
  130.6 0.7 broadcast_in_dim.2
  131.3 4.5 %all-to-all-start.3 = ((bf16[32,4,512]{2,1,0:T(4,128)(2,1)}), bf16[32,4,512]{2,1,0:T(4,128)(2,1)S(1)}, u32[]{:S(2)}, u32[]{:S(2)}) async-start(bf16[32,4,512]{2,1,0:T(4,128)(2,1)} %broadcast_in_dim.2), calls=%async_computation.3 | async-start | bytes 262144 | tf_op jit(solution)/shard_map/all_to_all | solution.py:363
  135.8 0.0 all-gather.5.cloned.1.call-done
  135.9 0.0 copy-start
  135.9 1.6 copy-done
  137.5 2.1 %shard_map.102 = bf16[512,512]{1,0:T(8,128)(2,1)} custom-call(s32[1]{0:T(128)} %bitcast.parity_ref, bf16[512,512]{1,0:T(8,128)(2,1)S(1)} %shard_map.99.res_ref, bf16[1024,512]{1,0:T(8,128)(2,1)S(1)} %get-tuple-element.26.one_ref, bf16[1024,512]{1,0:T(8,128)(2,1)S(1)} %get-tuple-element.27.two_ref, bf16[8,2,128,512]{3,2,1,0:T(8,128)(2,1)S(1)} %bitcast.13), custom_call_target="tpu_custom_call" | custom-call | flops 1073741824 | bytes 1048576 | tf_op jit(solution)/shard_map/pallas_call | solution.py:250
  139.5 13.5 %all-to-all-done.3 = bf16[32,4,512]{2,1,0:T(4,128)(2,1)S(1)} async-done(((bf16[32,4,512]{2,1,0:T(4,128)(2,1)}), bf16[32,4,512]{2,1,0:T(4,128)(2,1)S(1)}, u32[]{:S(2)}, u32[]{:S(2)}) %all-to-all-start.3) | async-done | bytes 131104 | tf_op jit(solution)/shard_map/all_to_all | solution.py:363
  153.0 0.8 reshape.35
  (4 shorter events, 0.1 us)
Async XLA Ops:
  7.2 60.2 %all-gather.3.cloned.1.call-start = ((), (), s32[]{:S(2)}) async-start(), calls=%async_computation.4 | async-start | bytes 2228224 | tf_op jit(solution)/shard_map/all_gather | solution.py:272
  7.9 128.0 %all-gather.5.cloned.1.call-start = ((), (), s32[]{:S(2)}) async-start(), calls=%async_computation.5 | async-start | bytes 2228224 | tf_op jit(solution)/shard_map/all_gather | solution.py:273
  7.9 33.0 %copy-start.1 = (s32[1,2,256]{2,1,0:T(2,128)S(1)}, s32[1,2,256]{2,1,0:T(2,128)}, u32[]{:S(2)}) copy-start(s32[1,2,256]{2,1,0:T(2,128)} %param.10) | copy-start | bytes 6148
  11.1 35.9 %copy-start.4 = (bf16[512,1536]{1,0:T(8,128)(2,1)S(1)}, bf16[512,1536]{1,0:T(8,128)(2,1)}, u32[]{:S(2)}) copy-start(bf16[512,1536]{1,0:T(8,128)(2,1)} %w_ref.1) | copy-start | bytes 4718596
  41.4 14.9 %collective-permute-start.1 = (bf16[2,272,512]{2,1,0:T(8,128)(2,1)S(1)}, bf16[2,272,512]{2,1,0:T(8,128)(2,1)S(1)}, u32[]{:S(2)}, u32[]{:S(2)}) collective-permute-start(bf16[2,272,512]{2,1,0:T(8,128)(2,1)S(1)} %shard_map.96.own_ref), channel_id=1, source_target_pairs={{0,1},{1,2},{2,3},{3,4},{4,5},{5,6},{6,7},{7,8},{8,9},{9,10},{10,1... | collective-permute-start | bytes 1671176 | tf_op jit(solution)/shard_map/ppermute | solution.py:301
  43.5 18.1 %collective-permute-start = (bf16[2,272,512]{2,1,0:T(8,128)(2,1)S(1)}, bf16[2,272,512]{2,1,0:T(8,128)(2,1)S(1)}, u32[]{:S(2)}, u32[]{:S(2)}) collective-permute-start(bf16[2,272,512]{2,1,0:T(8,128)(2,1)S(1)} %shard_map.96.own_ref), channel_id=1, source_target_pairs={{1,0},{2,1},{3,2},{4,3},{5,4},{6,5},{7,6},{8,7},{9,8},{10,9},{11,1... | collective-permute-start | bytes 1671176 | tf_op jit(solution)/shard_map/ppermute | solution.py:302
  47.1 1.1 copy-start.5
  48.1 1.0 copy-start.6
  52.1 9.5 %copy-start.7 = (bf16[512,512]{1,0:T(8,128)(2,1)}, bf16[512,512]{1,0:T(8,128)(2,1)S(1)}, u32[]{:S(2)}) copy-start(bf16[512,512]{1,0:T(8,128)(2,1)S(1)} %get-tuple-element.25.cot_ref) | copy-start | bytes 1572868
  61.6 5.8 %copy-start.8 = (bf16[512,512]{1,0:T(8,128)(2,1)S(1)}, bf16[512,512]{1,0:T(8,128)(2,1)}, u32[]{:S(2)}) copy-start(bf16[512,512]{1,0:T(8,128)(2,1)} %copy-done.7) | copy-start | bytes 1572868
  67.4 1.6 copy-start.2
  69.0 6.2 %copy-start.3 = (bf16[2048,512]{1,0:T(8,128)(2,1)S(1)}, bf16[2048,512]{1,0:T(8,128)(2,1)}, u32[]{:S(2)}) copy-start(bf16[2048,512]{1,0:T(8,128)(2,1)} %all-gather.3.cloned.1.call-done) | copy-start | bytes 6291460
  71.3 7.1 %collective-permute-start.2 = (bf16[2,8,64,512]{3,2,1,0:T(8,128)(2,1)S(1)}, bf16[2,8,64,512]{3,2,1,0:T(8,128)(2,1)S(1)}, u32[]{:S(2)}, u32[]{:S(2)}) collective-permute-start(bf16[2,8,64,512]{3,2,1,0:T(8,128)(2,1)S(1)} %get-tuple-element.29), channel_id=1, source_target_pairs={{0,1},{1,0},{2,3},{3,2},{4,5},{5,4},{6,7},{7,6},{8,9},{9,8},{10,11... | collective-permute-start | bytes 3145736 | tf_op jit(solution)/shard_map/ppermute | solution.py:338
  75.2 1.0 copy-start.9
  131.3 21.6 %all-to-all-start.3 = ((bf16[32,4,512]{2,1,0:T(4,128)(2,1)}), bf16[32,4,512]{2,1,0:T(4,128)(2,1)S(1)}, u32[]{:S(2)}, u32[]{:S(2)}) async-start(bf16[32,4,512]{2,1,0:T(4,128)(2,1)} %broadcast_in_dim.2), calls=%async_computation.3 | async-start | bytes 262144 | tf_op jit(solution)/shard_map/all_to_all | solution.py:363
  135.9 1.6 copy-start
Sparse Core Ops, SparseCore 0:
  10.1 52.3 all-gather.2
  64.7 50.9 all-gather.4
